TPU v7x, 128 devices: a whole 4x4x4 slice. The times are simulated.
128 devices in a mesh: band: 8 (over z_lo, y), grid: 16 (over x, z_hi, core).
Axes of the slice: x: 4, y: 4, z: 4 (z_hi: 2, z_lo: 2; z = z_hi * 2 + z_lo), core: 2. Of those that a mesh axis runs over, the one named last changes fastest.
Arguments:
- basis: float32 [128, 2, 1024, 128], P('band', None, 'grid'), may hold values from -6 to 6
- rotation: float32 [128, 16], replicated, may hold values from -0.5 to 0.5
- ritz_values: float32 [16], P('band'), may hold values from -1 to 3
- potential: float32 [128, 128, 128], P('grid'), may hold values from -4 to 4
- col_map: int32 [1024], replicated, may hold values from 0 to 16383, as said below
Outputs:
- resid: float32 [16, 2, 1024, 128], P('band', None, 'grid')
- h_resid: float32 [16, 2, 1024, 128], P('band', None, 'grid')
- intersection: float32 [128, 16], P('band')
Inputs may be any that keep to these rules, and one draw needn't show every extreme that they name: `col_map`: the 1024 positions are distinct.
All inputs are finite; a program needn't handle non-finite values.
Results may differ from a plain program's by a relative error of at most 0.0003.
Values sent between devices are 32-bit elements; how exact they have to be, the bound alone decides.
A program may use at most 64 MiB of HBM per device.

v0:
```python
import math

import jax
import jax.numpy as jnp
from jax import lax
from jax.sharding import PartitionSpec as P

N = 128


kinetic_coef = 2.0


def frequencies(values):
    return jnp.where(values >= N // 2, values - N, values)


def kinetic_table(positions):
    x_freq = frequencies(positions // N)
    y_freq = frequencies(positions % N)
    z_freq = frequencies(jnp.arange(N, dtype=jnp.int32))
    summed = (x_freq * x_freq + y_freq * y_freq)[:, None] + (z_freq * z_freq)[None, :]
    return kinetic_coef * summed.astype(jnp.float32) / float((N // 2) ** 2)


def phase_parts(row_index, sign, factor):
    indices = jnp.arange(N, dtype=jnp.int32)
    phases = row_index[:, None] * indices[None, :] % N
    angles = phases.astype(jnp.float32) * (2.0 * math.pi / N)
    return (jnp.cos(angles) * factor, sign * jnp.sin(angles) * factor)


def stacked_table(cosine, sine_part):
    return jnp.stack([jnp.stack([cosine, sine_part]), jnp.stack([-sine_part, cosine])])


def apply_hamiltonian(coeffs, potential, positions, kinetic):
    highest = lax.Precision.HIGHEST
    indices = jnp.arange(N, dtype=jnp.int32)
    x_index = positions // N
    y_index = positions % N
    inverse_z = stacked_table(*phase_parts(indices, 1.0, 1.0 / N))
    forward_z = stacked_table(*phase_parts(indices, -1.0, 1.0))
    inverse_x = stacked_table(*phase_parts(x_index, 1.0, 1.0 / N))
    forward_x = stacked_table(*phase_parts(x_index, -1.0, 1.0))
    inv_y_cos, inv_y_sin = phase_parts(y_index, 1.0, 1.0 / N)
    fwd_y_cos, fwd_y_sin = phase_parts(y_index, -1.0, 1.0)
    spread = jnp.einsum("bpcz,pqzk->bqkc", coeffs, inverse_z, precision=highest)
    slab_rows = lax.all_to_all(spread, "grid", split_axis=2, concat_axis=3, tiled=True)
    real_rows = slab_rows[:, 0][..., None]
    imag_rows = slab_rows[:, 1][..., None]
    weighted = jnp.stack(
        [
            real_rows * inv_y_cos - imag_rows * inv_y_sin,
            real_rows * inv_y_sin + imag_rows * inv_y_cos,
        ],
        axis=1,
    )
    planes = jnp.einsum("pqck,bpscm->bqskm", inverse_x, weighted, precision=highest)
    planes = planes * potential[None, None]
    lifted = jnp.einsum("pqck,bpskm->bqscm", forward_x, planes, precision=highest)
    picked_real = jnp.sum(lifted[:, 0] * fwd_y_cos - lifted[:, 1] * fwd_y_sin, axis=-1)
    picked_imag = jnp.sum(lifted[:, 0] * fwd_y_sin + lifted[:, 1] * fwd_y_cos, axis=-1)
    picked = jnp.stack([picked_real, picked_imag], axis=1)
    columns = lax.all_to_all(picked, "grid", split_axis=3, concat_axis=2, tiled=True)
    result = jnp.einsum("bpkc,pqkz->bqcz", columns, forward_z, precision=highest)
    return result + kinetic[None, None] * coeffs


def per_device(basis, rotation, ritz_values, potential, col_map):
    highest = lax.Precision.HIGHEST
    block_here = ritz_values.shape[0]
    col_here = basis.shape[2]
    total_columns = col_map.shape[0]
    local_map = lax.dynamic_slice_in_dim(col_map, lax.axis_index("grid") * col_here, col_here, 0)
    kinetic = kinetic_table(local_map)
    ritz_columns = lax.dynamic_slice_in_dim(
        rotation, lax.axis_index("band") * block_here, block_here, 1
    )
    ritz = jnp.einsum(
        "ij,ipcz->jpcz",
        ritz_columns,
        lax.all_gather(basis, "band", axis=0, tiled=True),
        precision=highest,
    )
    image = apply_hamiltonian(ritz, potential, col_map, kinetic)
    resid = (image - ritz_values[:, None, None, None] * ritz) / (1.0 + kinetic)
    h_resid = apply_hamiltonian(resid, potential, col_map, kinetic)
    partial_sum = jnp.einsum(
        "ipcz,jpcz->ij", basis, lax.all_gather(resid, "band", axis=0, tiled=True), precision=highest
    )
    intersection = lax.psum(partial_sum, "grid") / float(2 * N * total_columns)
    return (resid, h_resid, intersection)


def solution(mesh):
    placed = (P("band", None, "grid", None), P(), P("band"), P("grid", None, None), P())
    return jax.shard_map(
        per_device,
        mesh=mesh,
        in_specs=placed,
        out_specs=(P("band", None, "grid", None), P("band", None, "grid", None), P("band", None)),
        check_vma=False,
    )
```

profile of v0, /device:TPU:1, one launch (start us, length us, event | category | flops | bytes accessed | tf_op | source)
XLA Modules:
  0.0 326.9 jit_solution(2305158004463170636)
XLA Ops:
  12.2 3.3 %broadcast_multiply_fusion.1 = (f32[1,1024,128]{2,1,0:T(8,128)S(1)}, f32[1,1024,128]{2,1,0:T(8,128)}, f32[1,1024,128]{2,1,0:T(8,128)S(1)}, f32[1,1024,128]{2,1,0...) fusion(s32[1024]{0:T(1024)S(1)} %get-tuple-element.48), kind=kLoop, calls=%fused_computation.67 | loop fusion | flops 2490368 | bytes 3149824 | tf_op jit(solution)/shard_map/mul | solution.py:30
  17.7 3.1 fusion.31
  20.8 84.6 %all-gather.3.cloned.1.call-done = f32[128,2,64,128]{3,0,2,1:T(8,128)} async-done(((f32[16,2,64,128]{3,0,2,1:T(8,128)}), f32[128,2,64,128]{3,0,2,1:T(8,128)}) %all-gather.3.cloned.1.call-update) | async-done | bytes 8388624 | tf_op jit(solution)/shard_map/all_gather | solution.py:83
  105.4 6.3 %fusion.53 = f32[2,2,64,128]{3,0,2,1:T(2,128)S(1)} fusion(f32[128,2,64,128]{3,0,2,1:T(8,128)} %all-gather.3.cloned.1.call-done, f32[128,16]{0,1:T(8,128)S(1)} %copy-done, s32[]{:T(128)S(6)} %select_n.162), kind=kOutput, calls=%fused_computation.132 | convolution fusion | flops 50331648 | bytes 8520708 | tf_op jit(solution)/shard_map/ij,ipcz->jpcz/dot_general | solution.py:80
  113.2 7.8 %all-to-all-start = ((f32[16,1,2048]{2,1,0:T(1,128)}), f32[16,1,2048]{2,1,0:T(1,128)S(1)}, u32[]{:S(2)}, u32[]{:S(2)}) async-start(f32[16,1,2048]{2,1,0:T(1,128)} %reshape.510), calls=%async_computation | async-start | bytes 262144 | tf_op jit(solution)/shard_map/all_to_all | solution.py:49
  124.7 3.8 %all-to-all-done = f32[16,1,2048]{2,1,0:T(1,128)S(1)} async-done(((f32[16,1,2048]{2,1,0:T(1,128)}), f32[16,1,2048]{2,1,0:T(1,128)S(1)}, u32[]{:S(2)}, u32[]{:S(2)}) %all-to-all-start) | async-done | bytes 131104 | tf_op jit(solution)/shard_map/all_to_all | solution.py:49
  133.5 3.7 %multiply_subtract_fusion.1 = (f32[2,1,8,1024,128]{3,4,1,2,0:T(8,128)S(1)}, f32[2,1,8,1024,128]{3,4,1,2,0:T(8,128)S(1)}) fusion(f32[1024,128]{0,1:T(8,128)} %get-tuple-element.41, f32[2,8,1024]{2,1,0:T(8,128)S(1)} %get-tuple-element.33, f32[1024,128]{0,1:T(8,128)} %get-tuple-element.39, f32[2,8,1024]{2,1,0:T(8,128)S(1)} %get-tuple-element.32), kind=kLoop, calls=%fused_computation.19 | loop fusion | flops 12582912 | bytes 17956864 | tf_op jit(solution)/shard_map/sub | solution.py:54
  137.3 14.0 %fusion = f32[2,8,128,2,128,1]{4,2,5,3,1,0:T(8,128)S(1)} fusion(f32[2,1,8,1024,128]{3,4,1,2,0:T(8,128)S(1)} %get-tuple-element.25, f32[2,1,8,1024,128]{3,4,1,2,0:T(8,128)S(1)} %get-tuple-element.24, f32[1,2,1024,128]{3,2,0,1:T(8,128)S(1)} %copy-done.11, f32[1,2,1024,128]{3,2,0,1:T(8,128)S(1)} %copy-done.9), kind=kOutput, calls=%fused_computation.1 | convolution fusion | flops 12889620480 | bytes 20971520 | tf_op jit(solution)/shard_map/pqck,bpscm->bqskm/dot_general | solution.py:59
  151.3 13.9 %convolution_bitcast_fusion = f32[2,2,8,1024,128]{3,4,1,2,0:T(8,128)S(1)} fusion(f32[2,8,128,2,128,1]{4,2,5,3,1,0:T(8,128)S(1)} %fusion, f32[8,128,128]{1,2,0:T(8,128)S(1)} %copy.131, f32[1,2,1024,128]{3,2,1,0:T(8,128)S(1)} %get-tuple-element.27, f32[1,2,1024,128]{3,2,1,0:T(8,128)S(1)} %get-tuple-element.26), kind=kOutput, calls=%fused_computation.20 | convolution fusion | flops 12885950464 | bytes 21495808 | tf_op jit(solution)/shard_map/pqck,bpskm->bqscm/dot_general | solution.py:61
  170.0 5.0 %reshape.512 = f32[16,1,2048]{2,1,0:T(1,128)} reshape(f32[1024,2,2,8]{3,2,1,0:T(2,128)} %bitcast.212) | data formatting | bytes 262144
  175.0 4.3 %all-to-all-start.1 = ((f32[16,1,2048]{2,1,0:T(1,128)}), f32[16,1,2048]{2,1,0:T(1,128)}, u32[]{:S(2)}, u32[]{:S(2)}) async-start(f32[16,1,2048]{2,1,0:T(1,128)} %reshape.512), calls=%async_computation.1 | async-start | bytes 262144 | tf_op jit(solution)/shard_map/all_to_all | solution.py:65
  180.5 6.6 %all-to-all-done.1 = f32[16,1,2048]{2,1,0:T(1,128)} async-done(((f32[16,1,2048]{2,1,0:T(1,128)}), f32[16,1,2048]{2,1,0:T(1,128)}, u32[]{:S(2)}, u32[]{:S(2)}) %all-to-all-start.1) | async-done | bytes 131104 | tf_op jit(solution)/shard_map/all_to_all | solution.py:65
  189.6 5.4 %reshape.513 = f32[1024,2,2,8]{3,2,1,0:T(2,128)} reshape(f32[16,2048]{1,0:T(8,128)} %reduce.1) | data formatting | bytes 262144
  195.0 3.8 %copy.184 = f32[2,2,8,16,64]{4,2,3,1,0:T(8,128)} copy(f32[2,2,8,16,64]{2,1,0,4,3:T(2,128)} %bitcast.213) | data formatting | bytes 262144 | tf_op jit(solution)/shard_map/all_to_all | solution.py:65
  207.6 4.3 %all-to-all-start.2 = ((f32[16,1,2048]{2,1,0:T(1,128)}), f32[16,1,2048]{2,1,0:T(1,128)}, u32[]{:S(2)}, u32[]{:S(2)}) async-start(f32[16,1,2048]{2,1,0:T(1,128)} %reshape.514), calls=%async_computation.2 | async-start | bytes 262144 | tf_op jit(solution)/shard_map/all_to_all | solution.py:49
  212.7 7.1 %all-to-all-done.2 = f32[16,1,2048]{2,1,0:T(1,128)} async-done(((f32[16,1,2048]{2,1,0:T(1,128)}), f32[16,1,2048]{2,1,0:T(1,128)}, u32[]{:S(2)}, u32[]{:S(2)}) %all-to-all-start.2) | async-done | bytes 131104 | tf_op jit(solution)/shard_map/all_to_all | solution.py:49
  225.4 3.7 %multiply_subtract_fusion = (f32[2,1,8,1024,128]{3,4,1,2,0:T(8,128)S(1)}, f32[2,1,8,1024,128]{3,4,1,2,0:T(8,128)S(1)}) fusion(f32[2,8,1024]{2,1,0:T(8,128)S(1)} %get-tuple-element.31, f32[2,8,1024]{2,1,0:T(8,128)S(1)} %get-tuple-element.30, f32[1024,128]{0,1:T(8,128)} %get-tuple-element.41, f32[1024,128]{0,1:T(8,128)} %get-tuple-element.39), kind=kLoop, calls=%fused_computation.15 | loop fusion | flops 12582912 | bytes 17956864 | tf_op jit(solution)/shard_map/sub | solution.py:54
  229.2 14.0 %fusion.3 = f32[2,8,128,2,128,1]{4,2,5,3,1,0:T(8,128)S(1)} fusion(f32[2,1,8,1024,128]{3,4,1,2,0:T(8,128)S(1)} %get-tuple-element.23, f32[2,1,8,1024,128]{3,4,1,2,0:T(8,128)S(1)} %get-tuple-element.22, f32[1,2,1024,128]{3,2,0,1:T(8,128)S(1)} %copy-done.12, f32[1,2,1024,128]{3,2,0,1:T(8,128)S(1)} %copy-done.10), kind=kOutput, calls=%fused_computation.5 | convolution fusion | flops 12889620480 | bytes 20971520 | tf_op jit(solution)/shard_map/pqck,bpscm->bqskm/dot_general | solution.py:59
  243.1 13.7 %convolution_bitcast_fusion.1 = f32[2,2,8,1024,128]{3,4,2,0,1:T(8,128)S(1)} fusion(f32[2,8,128,2,128,1]{4,2,5,3,1,0:T(8,128)S(1)} %fusion.3, f32[8,128,128]{1,2,0:T(8,128)S(1)} %copy.131, f32[1,2,1024,128]{3,2,1,0:T(8,128)S(1)} %get-tuple-element.27, f32[1,2,1024,128]{3,2,1,0:T(8,128)S(1)} %get-tuple-element.26), kind=kOutput, calls=%fused_computation.21 | convolution fusion | flops 12885950464 | bytes 21495808 | tf_op jit(solution)/shard_map/pqck,bpskm->bqscm/dot_general | solution.py:61
  260.8 3.4 %reshape.516 = f32[16,1,2048]{2,1,0:T(1,128)S(1)} reshape(f32[1024,2,2,8]{3,2,1,0:T(2,128)S(1)} %bitcast.214) | data formatting | bytes 262144
  264.1 10.6 %all_to_all.72 = f32[16,1,2048]{2,1,0:T(1,128)S(1)} all-to-all(f32[16,1,2048]{2,1,0:T(1,128)S(1)} %reshape.516), channel_id=1, replica_groups=mesh['band'=8,'grid'=16] {'grid'}, dimensions={0} | all-to-all | bytes 262144 | tf_op jit(solution)/shard_map/all_to_all | solution.py:65
  275.7 3.2 reshape.517
  281.8 4.0 %convolution_bitcast_fusion.6 = f32[16,16]{0,1:T(8,128)S(1)} fusion(f32[16,2,64,128]{3,2,1,0:T(8,128)} %param.5, f32[16,2,64,128]{3,2,1,0:T(8,128)} %all-gather.5.cloned.1.call-done), kind=kOutput, calls=%fused_computation.33 | convolution fusion | flops 50331648 | bytes 2098176 | tf_op jit(solution)/shard_map/ipcz,jpcz->ij/dot_general | solution.py:89
  285.8 33.4 %psum.7 = f32[16,16]{0,1:T(8,128)S(1)} all-reduce(f32[16,16]{0,1:T(8,128)S(1)} %convolution_bitcast_fusion.6), channel_id=1, replica_groups=mesh['band'=8,'grid'=16] {'grid'}, use_global_device_ids=true, to_apply=%region_4.5 | all-reduce | flops 256 | bytes 2048 | tf_op jit(solution)/shard_map/psum | solution.py:92
  (85 shorter events, 49.3 us)
Async XLA Ops:
  7.2 98.2 %copy-start = (f32[128,16]{0,1:T(8,128)S(1)}, f32[128,16]{0,1:T(8,128)}, u32[]{:S(2)}) copy-start(f32[128,16]{0,1:T(8,128)} %param.6) | copy-start | bytes 24580
  7.2 98.2 %all-gather.3.cloned.1.call-start = ((), (), s32[]{:S(2)}) async-start(), calls=%async_computation.4 | async-start | bytes 9437184 | tf_op jit(solution)/shard_map/all_gather | solution.py:83
  11.4 100.3 %copy-start.4 = (f32[1,2,128,128]{3,2,0,1:T(8,128)}, f32[1,2,128,128]{3,2,0,1:T(8,128)S(1)}, u32[]{:S(2)}) copy-start(f32[1,2,128,128]{3,2,0,1:T(8,128)S(1)} %get-tuple-element.36) | copy-start | bytes 393220
  11.4 100.3 %copy-start.5 = (f32[1,2,128,128]{3,2,0,1:T(8,128)}, f32[1,2,128,128]{3,2,0,1:T(8,128)S(1)}, u32[]{:S(2)}) copy-start(f32[1,2,128,128]{3,2,0,1:T(8,128)S(1)} %get-tuple-element.37) | copy-start | bytes 393220
  113.2 15.4 %all-to-all-start = ((f32[16,1,2048]{2,1,0:T(1,128)}), f32[16,1,2048]{2,1,0:T(1,128)S(1)}, u32[]{:S(2)}, u32[]{:S(2)}) async-start(f32[16,1,2048]{2,1,0:T(1,128)} %reshape.510), calls=%async_computation | async-start | bytes 262144 | tf_op jit(solution)/shard_map/all_to_all | solution.py:49
  133.5 3.7 %copy-start.9 = (f32[1,2,1024,128]{3,2,0,1:T(8,128)S(1)}, f32[1,2,1024,128]{3,2,0,1:T(8,128)}, u32[]{:S(2)}) copy-start(f32[1,2,1024,128]{3,2,0,1:T(8,128)} %get-tuple-element.28) | copy-start | bytes 3145732
  133.5 3.7 %copy-start.11 = (f32[1,2,1024,128]{3,2,0,1:T(8,128)S(1)}, f32[1,2,1024,128]{3,2,0,1:T(8,128)}, u32[]{:S(2)}) copy-start(f32[1,2,1024,128]{3,2,0,1:T(8,128)} %get-tuple-element.29) | copy-start | bytes 3145732
  151.2 13.9 %copy-start.2 = (f32[1024,128]{0,1:T(8,128)S(1)}, f32[1024,128]{0,1:T(8,128)}, u32[]{:S(2)}) copy-start(f32[1024,128]{0,1:T(8,128)} %get-tuple-element.40) | copy-start | bytes 1572868
  167.7 32.7 %copy-start.14 = (f32[2]{0:T(128)S(1)}, f32[2]{0:T(128)}, u32[]{:S(2)}) copy-start(f32[2]{0:T(128)} %param.7) | copy-start | bytes 28
  175.0 12.1 %all-to-all-start.1 = ((f32[16,1,2048]{2,1,0:T(1,128)}), f32[16,1,2048]{2,1,0:T(1,128)}, u32[]{:S(2)}, u32[]{:S(2)}) async-start(f32[16,1,2048]{2,1,0:T(1,128)} %reshape.512), calls=%async_computation.1 | async-start | bytes 262144 | tf_op jit(solution)/shard_map/all_to_all | solution.py:65
  201.3 0.7 copy-start.7
  202.0 10.0 %copy-start.6 = (f32[2,2,64,128]{3,2,1,0:T(8,128)}, f32[2,2,64,128]{3,2,1,0:T(8,128)S(1)}, u32[]{:S(2)}) copy-start(f32[2,2,64,128]{3,2,1,0:T(8,128)S(1)} %copy.155) | copy-start | bytes 393220
  207.6 12.2 %all-to-all-start.2 = ((f32[16,1,2048]{2,1,0:T(1,128)}), f32[16,1,2048]{2,1,0:T(1,128)}, u32[]{:S(2)}, u32[]{:S(2)}) async-start(f32[16,1,2048]{2,1,0:T(1,128)} %reshape.514), calls=%async_computation.2 | async-start | bytes 262144 | tf_op jit(solution)/shard_map/all_to_all | solution.py:49
  212.0 69.8 %all-gather.5.cloned.1.call-start = ((), (), s32[]{:S(2)}) async-start(), calls=%async_computation.5 | async-start | bytes 1179648 | tf_op jit(solution)/shard_map/all_gather | solution.py:90
  225.4 3.7 %copy-start.10 = (f32[1,2,1024,128]{3,2,0,1:T(8,128)S(1)}, f32[1,2,1024,128]{3,2,0,1:T(8,128)}, u32[]{:S(2)}) copy-start(f32[1,2,1024,128]{3,2,0,1:T(8,128)} %get-tuple-element.28) | copy-start | bytes 3145732
  225.4 3.7 %copy-start.12 = (f32[1,2,1024,128]{3,2,0,1:T(8,128)S(1)}, f32[1,2,1024,128]{3,2,0,1:T(8,128)}, u32[]{:S(2)}) copy-start(f32[1,2,1024,128]{3,2,0,1:T(8,128)} %get-tuple-element.29) | copy-start | bytes 3145732
  243.1 13.7 %copy-start.3 = (f32[1024,128]{0,1:T(8,128)S(1)}, f32[1024,128]{0,1:T(8,128)}, u32[]{:S(2)}) copy-start(f32[1024,128]{0,1:T(8,128)} %get-tuple-element.40) | copy-start | bytes 1572868
  256.8 63.0 %copy-start.1 = (f32[128,16]{0,1:T(8,128)S(1)}, f32[128,16]{0,1:T(8,128)}, u32[]{:S(2)}) copy-start(f32[128,16]{0,1:T(8,128)} %param.6) | copy-start | bytes 24580
  259.4 21.5 %copy-start.8 = (f32[2,2,64,128]{3,0,2,1:T(2,128)S(1)}, f32[2,2,64,128]{3,0,2,1:T(2,128)}, u32[]{:S(2)}) copy-start(f32[2,2,64,128]{3,0,2,1:T(2,128)} %copy-done.7) | copy-start | bytes 393220
  259.4 21.5 %copy-start.13 = (f32[64,128]{1,0:T(8,128)S(1)}, f32[64,128]{1,0:T(8,128)}, u32[]{:S(2)}) copy-start(f32[64,128]{1,0:T(8,128)} %get-tuple-element.50) | copy-start | bytes 98308
Sparse Core Ops, SparseCore 0:
  10.2 95.1 all-gather.2
  215.0 32.8 all-gather.4
where the time goes:
time: 333 us; the launch traced here: 327 us
  waiting for transfers between devices  103 us (31%)
  matrix products  70.2 us (21%)
  blocking collectives  44 us (13%)
  local copies, waits for them, and re-layouts  43.8 us (13%)
  other arithmetic  34.9 us (10%)
  starting transfers between devices  16.5 us (5%)
  between operations  14.7 us (4%)
    all_gather x1, waiting for transfers between devices, per_device(): lax.all_gather(basis, 'band', axis=0, tiled=True)  84.6 us
    psum x1, blocking collectives, per_device(): intersection = lax.psum(partial_sum, 'grid') / float(2 * N * total_columns)  33.4 us
    dot_general x2, matrix products, apply_hamiltonian(): jnp.einsum('pqck,bpscm->bqskm', inverse_x, weighted, precision=highest)  28 us
    unnamed x43, local copies, waits for them, and re-layouts  27.9 us
    dot_general x2, matrix products, apply_hamiltonian(): jnp.einsum('pqck,bpskm->bqscm', forward_x, planes, precision=highest)  27.5 us
    all_to_all x2, starting transfers between devices, apply_hamiltonian(): lax.all_to_all(spread, 'grid', split_axis=2, concat_axis=3, tiled=True)  12.1 us
    all_to_all x2, waiting for transfers between devices, apply_hamiltonian(): lax.all_to_all(spread, 'grid', split_axis=2, concat_axis=3, tiled=True)  10.9 us
    all_to_all x1, blocking collectives, apply_hamiltonian(): lax.all_to_all(picked, 'grid', split_axis=3, concat_axis=2, tiled=True)  10.6 us
  transfers between devices with their start and end apart: 5, of which 4 were waited for; matrix products, arithmetic and copies ran while one was open for 20% of the time, Pallas kernels for 0%

commit v1 on v0

v1 whole, which is shorter than its diff:
```python
import functools

import jax
import jax.numpy as jnp
import ml_dtypes
import numpy as np
from jax import lax
from jax.experimental import pallas as pl
from jax.experimental.pallas import tpu as pltpu
from jax.sharding import PartitionSpec as P

MESH = pl.DeviceIdType.MESH
N = 128
HALF = 64
LOW = 32
TOP = N // LOW
KINETIC_COEF = 2.0
F32 = jnp.float32
BF16 = jnp.bfloat16


def angle_tables():
    index = np.arange(N)
    angles = 2.0 * np.pi * (np.outer(index, index) % N) / N
    return np.cos(angles), np.sin(angles)


def split_table(table):
    high = table.astype(ml_dtypes.bfloat16)
    low = (table - high.astype(np.float64)).astype(ml_dtypes.bfloat16)
    return np.stack([high, low])


def make_tables():
    cosine, sine = angle_tables()
    inverse_z = (np.concatenate([cosine, sine], axis=1) / N).astype(np.float32)
    forward_z = np.concatenate([cosine, sine], axis=0).astype(np.float32)
    inverse = np.block([[cosine, sine], [-sine, cosine]]) / N
    forward = np.block([[cosine, -sine], [sine, cosine]])
    tables = np.concatenate(
        [split_table(inverse), split_table(inverse.T), split_table(forward), split_table(forward.T)]
    )
    return inverse_z, forward_z, tables


RIGHT_INV, LEFT_INV, RIGHT_FWD, LEFT_FWD = 0, 2, 4, 6


def split(value):
    high = value.astype(BF16)
    return high, (value - high.astype(F32)).astype(BF16)


def dot(left, right):
    return jnp.dot(left, right, preferred_element_type=F32)


def wait_bytes(view, sem):
    pltpu.make_async_copy(view, view, sem).wait()


def kernel(
    n_band, n_grid, total,
    basis_ref, rot_ref, ritz_val_ref, pot_ref, map_ref, tzi_ref, tzf_ref, tab_ref,
    resid_ref, hres_ref, inter_ref,
    part, rs, coeff, kin, onehot, onehot_t, mask, tmp,
    send_f, recv_f, send_b, recv_b,
    vals, wide_h, wide_l, rows_h, rows_l, cols_h, cols_l, read_h, read_l,
    gath, acc, psend, precv,
    rs_send, rs_recv, f_send, f_recv, b_send, b_recv, g_send, g_recv, p_send, p_recv,
):
    slabs = N // n_grid
    chunks = total // N
    n_sub = basis_ref.shape[0]
    my_band = lax.axis_index("band")
    my_grid = lax.axis_index("grid")

    barrier = pltpu.get_barrier_semaphore()

    def greet_band(step, carry):
        peer = lax.rem(my_band + step, n_band)
        pl.semaphore_signal(barrier, inc=1, device_id=(peer, my_grid), device_id_type=MESH)
        return carry

    def greet_grid(step, carry):
        peer = lax.rem(my_grid + step, n_grid)
        pl.semaphore_signal(barrier, inc=1, device_id=(my_band, peer), device_id_type=MESH)
        return carry

    lax.fori_loop(1, n_band, greet_band, 0)
    lax.fori_loop(1, n_grid, greet_grid, 0)
    pl.semaphore_wait(barrier, n_band - 1 + n_grid - 1)

    def partial_of(owner, which):
        column = owner * 2 + which
        row = my_band * n_sub
        value = rot_ref[row, column] * basis_ref[0]
        for i in range(1, n_sub):
            value = value + rot_ref[row + i, column] * basis_ref[i]
        return value

    for which in range(2):
        def send_partial(step, carry, which=which):
            owner = lax.rem(my_band + step, n_band)
            part[which, owner] = partial_of(owner, which)
            pltpu.make_async_remote_copy(
                src_ref=part.at[which, owner],
                dst_ref=rs.at[which, my_band],
                send_sem=rs_send.at[which],
                recv_sem=rs_recv.at[which],
                device_id=(owner, my_grid),
                device_id_type=MESH,
            ).start()
            return carry

        lax.fori_loop(1, n_band, send_partial, 0)
        rs[which, my_band] = partial_of(my_band, which)

    lane_c = lax.broadcasted_iota(jnp.int32, (TOP * N, N), 0)
    lane_r = lax.broadcasted_iota(jnp.int32, (LOW, N), 0)
    for j in range(chunks):
        span = slice(j * N, (j + 1) * N)
        pos = map_ref[j:j + 1, :]
        x = lax.shift_right_logical(pos, 7)
        y = lax.bitwise_and(pos, N - 1)
        high = lax.shift_right_logical(x, 5) * N + y
        hit = jnp.where(lane_c == jnp.broadcast_to(high, lane_c.shape), 1.0, 0.0)
        onehot_t[:, span] = hit.astype(BF16)
        for t in range(TOP):
            onehot[span, t * N:(t + 1) * N] = hit[t * N:(t + 1) * N].T.astype(BF16)
        low = jnp.broadcast_to(lax.bitwise_and(x, LOW - 1), lane_r.shape)
        mask[:, span] = jnp.where(lane_r == low, 1.0, 0.0)

    mine = map_ref[pl.ds(my_grid // 2, 1), :].astype(F32)
    tmp[...] = jnp.broadcast_to(mine, (N, N)).T
    here = tmp[pl.ds(pl.multiple_of(lax.rem(my_grid, 2) * HALF, HALF), HALF), :].astype(jnp.int32)
    fx = lax.shift_right_logical(here, 7)
    fy = lax.bitwise_and(here, N - 1)
    fz = lax.broadcasted_iota(jnp.int32, (HALF, N), 1)
    fx = jnp.where(fx >= HALF, fx - N, fx)
    fy = jnp.where(fy >= HALF, fy - N, fy)
    fz = jnp.where(fz >= HALF, fz - N, fz)
    squares = (fx * fx + fy * fy + fz * fz).astype(F32)
    kinetic = squares * (KINETIC_COEF / float((N // 2) ** 2))
    kin[0:HALF] = kinetic
    kin[HALF:N] = kinetic

    lane = lax.broadcasted_iota(jnp.int32, (slabs, N), 1)
    first = lane < HALF

    def exchange(send, recv, send_sem, recv_sem, unit):
        def go(step, carry):
            peer = lax.rem(my_grid + step, n_grid)
            there = pl.multiple_of(peer * slabs, slabs)
            here_at = pl.multiple_of(my_grid * slabs, slabs)
            pltpu.make_async_remote_copy(
                src_ref=send.at[unit, pl.ds(there, slabs)],
                dst_ref=recv.at[unit, pl.ds(here_at, slabs)],
                send_sem=send_sem.at[unit],
                recv_sem=recv_sem.at[unit],
                device_id=(my_band, peer),
                device_id_type=MESH,
            ).start()
            return carry

        lax.fori_loop(1, n_grid, go, 0)
        own = pl.multiple_of(my_grid * slabs, slabs)
        recv[unit, pl.ds(own, slabs)] = send[unit, pl.ds(own, slabs)]

    def wait_exchange(recv, sem, unit):
        wait_bytes(recv.at[unit, pl.ds(0, N - slabs)], sem.at[unit])

    def spread(value, unit):
        real, imag = value[0:HALF], value[HALF:N]
        right = jnp.concatenate(
            [jnp.concatenate([real, -imag], axis=1), jnp.concatenate([imag, real], axis=1)], axis=0
        )
        send_f[unit] = lax.dot_general(
            tzi_ref[...], right, (((1,), (1,)), ((), ())),
            precision=lax.Precision.HIGHEST, preferred_element_type=F32,
        )
        exchange(send_f, recv_f, f_send, f_recv, unit)

    def ritz_ready(which):
        wait_bytes(rs.at[which, pl.ds(0, n_band - 1)], rs_recv.at[which])
        value = rs[which, 0]
        for d in range(1, n_band):
            value = value + rs[which, d]
        coeff[which] = value
        spread(value, which)

    def plane_inverse(unit):
        wait_exchange(recv_f, f_recv, unit)
        for j in range(chunks):
            span = slice(j * N, (j + 1) * N)
            left = recv_f[unit, 2 * j * slabs:(2 * j + 1) * slabs]
            right = recv_f[unit, (2 * j + 1) * slabs:(2 * j + 2) * slabs]
            vals[0:slabs, span] = jnp.where(first, left, pltpu.roll(right, HALF, 1))
            vals[slabs:2 * slabs, span] = jnp.where(first, pltpu.roll(left, HALF, 1), right)
        chosen = mask[...] > 0.5
        for k in range(2 * slabs):
            row = vals[k:k + 1, :]
            high = row.astype(BF16).astype(F32)
            low = row - high
            span = slice(k * LOW, (k + 1) * LOW)
            wide_h[span] = jnp.where(chosen, jnp.broadcast_to(high, chosen.shape), 0.0).astype(BF16)
            wide_l[span] = jnp.where(chosen, jnp.broadcast_to(low, chosen.shape), 0.0).astype(BF16)
        for wide, rows in ((wide_h, rows_h), (wide_l, rows_l)):
            placed = dot(wide[...], onehot[...]).astype(BF16)
            for q in range(2):
                for s in range(slabs):
                    k = q * slabs + s
                    for t in range(TOP):
                        rows[s * N + t * LOW:s * N + (t + 1) * LOW, q * N:(q + 1) * N] = placed[
                            k * LOW:(k + 1) * LOW, t * N:(t + 1) * N
                        ]
        along_y = (
            dot(rows_h[...], tab_ref[RIGHT_INV])
            + dot(rows_h[...], tab_ref[RIGHT_INV + 1])
            + dot(rows_l[...], tab_ref[RIGHT_INV])
        )
        high, low = split(along_y)
        for q in range(2):
            for s in range(slabs):
                cols_h[q * N:(q + 1) * N, s * N:(s + 1) * N] = high[s * N:(s + 1) * N, q * N:(q + 1) * N]
                cols_l[q * N:(q + 1) * N, s * N:(s + 1) * N] = low[s * N:(s + 1) * N, q * N:(q + 1) * N]
        field = (
            dot(tab_ref[LEFT_INV], cols_h[...])
            + dot(tab_ref[LEFT_INV + 1], cols_h[...])
            + dot(tab_ref[LEFT_INV], cols_l[...])
        )
        for s in range(slabs):
            span = slice(s * N, (s + 1) * N)
            here_pot = pot_ref[s]
            for q in range(2):
                high, low = split(field[q * N:(q + 1) * N, span] * here_pot)
                cols_h[q * N:(q + 1) * N, span] = high
                cols_l[q * N:(q + 1) * N, span] = low

    def plane_forward(unit):
        along_x = (
            dot(tab_ref[LEFT_FWD], cols_h[...])
            + dot(tab_ref[LEFT_FWD + 1], cols_h[...])
            + dot(tab_ref[LEFT_FWD], cols_l[...])
        )
        high, low = split(along_x)
        for q in range(2):
            for s in range(slabs):
                rows_h[s * N:(s + 1) * N, q * N:(q + 1) * N] = high[q * N:(q + 1) * N, s * N:(s + 1) * N]
                rows_l[s * N:(s + 1) * N, q * N:(q + 1) * N] = low[q * N:(q + 1) * N, s * N:(s + 1) * N]
        along_y = (
            dot(rows_h[...], tab_ref[RIGHT_FWD])
            + dot(rows_h[...], tab_ref[RIGHT_FWD + 1])
            + dot(rows_l[...], tab_ref[RIGHT_FWD])
        )
        high, low = split(along_y)
        for q in range(2):
            for s in range(slabs):
                k = q * slabs + s
                for t in range(TOP):
                    at = slice(s * N + t * LOW, s * N + (t + 1) * LOW)
                    read_h[k * LOW:(k + 1) * LOW, t * N:(t + 1) * N] = high[at, q * N:(q + 1) * N]
                    read_l[k * LOW:(k + 1) * LOW, t * N:(t + 1) * N] = low[at, q * N:(q + 1) * N]
        picked = dot(read_h[...], onehot_t[...]) + dot(read_l[...], onehot_t[...])
        for k in range(2 * slabs):
            vals[k:k + 1, :] = jnp.sum(
                picked[k * LOW:(k + 1) * LOW] * mask[...], axis=0, keepdims=True
            )
        for j in range(chunks):
            span = slice(j * N, (j + 1) * N)
            real = vals[0:slabs, span]
            imag = vals[slabs:2 * slabs, span]
            send_b[unit, 2 * j * slabs:(2 * j + 1) * slabs] = jnp.where(
                first, real, pltpu.roll(imag, HALF, 1)
            )
            send_b[unit, (2 * j + 1) * slabs:(2 * j + 2) * slabs] = jnp.where(
                first, pltpu.roll(real, HALF, 1), imag
            )
        exchange(send_b, recv_b, b_send, b_recv, unit)

    def finish(unit, which):
        wait_exchange(recv_b, b_recv, unit)
        turned = recv_b[unit].T
        real, imag = turned[0:HALF], turned[HALF:N]
        left = jnp.concatenate(
            [jnp.concatenate([real, imag], axis=1), jnp.concatenate([imag, -real], axis=1)], axis=0
        )
        value = jnp.dot(
            left, tzf_ref[...], precision=lax.Precision.HIGHEST, preferred_element_type=F32
        )
        return value + kin[...] * coeff[which]

    def residual(unit):
        which = unit
        image = finish(unit, which)
        value = (image - ritz_val_ref[which] * coeff[which]) / (1.0 + kin[...])
        coeff[which] = value
        resid_ref[which] = value
        gath[which, my_band] = value
        spread(value, unit + 2)

        def go(step, carry):
            owner = lax.rem(my_band + step, n_band)
            pltpu.make_async_remote_copy(
                src_ref=gath.at[which, my_band],
                dst_ref=gath.at[which, my_band],
                send_sem=g_send.at[which],
                recv_sem=g_recv.at[which],
                device_id=(owner, my_grid),
                device_id_type=MESH,
            ).start()
            return carry

        lax.fori_loop(1, n_band, go, 0)

    def products(which):
        wait_bytes(gath.at[which, pl.ds(0, n_band - 1)], g_recv.at[which])

        def of_owner(owner, carry):
            there = gath[which, owner]
            for i in range(n_sub):
                both = basis_ref[i] * there
                acc[which, owner, i] = jnp.sum(both.reshape(N // 8, 8, N), axis=0)
            return carry

        lax.fori_loop(0, n_band, of_owner, 0)

    def send_products():
        count = 2 * n_band * n_sub
        summed = jnp.sum(acc[...].reshape(count, 8, N), axis=1)
        ones = jnp.ones((N, N), F32)
        spread_sum = jnp.dot(
            summed, ones, precision=lax.Precision.HIGHEST, preferred_element_type=F32
        )
        row = lax.broadcasted_iota(jnp.int32, (count, N), 0)
        column = lax.broadcasted_iota(jnp.int32, (count, N), 1)
        owner = lax.rem(row // n_sub, n_band)
        which = row // (n_sub * n_band)
        spread_sum = jnp.where(column == 2 * owner + which, spread_sum, 0.0)
        total_sum = spread_sum[0:n_sub]
        for k in range(1, 2 * n_band):
            total_sum = total_sum + spread_sum[k * n_sub:(k + 1) * n_sub]
        psend[...] = total_sum
        precv[my_grid] = total_sum

        def go(step, carry):
            peer = lax.rem(my_grid + step, n_grid)
            pltpu.make_async_remote_copy(
                src_ref=psend,
                dst_ref=precv.at[my_grid],
                send_sem=p_send,
                recv_sem=p_recv,
                device_id=(my_band, peer),
                device_id_type=MESH,
            ).start()
            return carry

        lax.fori_loop(1, n_grid, go, 0)

    ritz_ready(0)
    plane_inverse(0)
    ritz_ready(1)
    plane_forward(0)

    plane_inverse(1)
    residual(0)
    plane_forward(1)

    plane_inverse(2)
    residual(1)
    plane_forward(2)

    plane_inverse(3)
    hres_ref[0] = finish(2, 0)
    products(0)
    products(1)
    send_products()
    plane_forward(3)
    wait_bytes(precv.at[pl.ds(0, n_grid - 1)], p_recv)
    value = precv[0]
    for d in range(1, n_grid):
        value = value + precv[d]
    inter_ref[...] = value[:, 0:2 * n_band] / float(2 * N * total)
    hres_ref[1] = finish(3, 1)

    for which in range(2):
        wait_bytes(part.at[which, pl.ds(0, n_band - 1)], rs_send.at[which])
        wait_bytes(gath.at[which, pl.ds(0, n_band - 1)], g_send.at[which])
    for unit in range(4):
        wait_bytes(send_f.at[unit, pl.ds(0, N - slabs)], f_send.at[unit])
        wait_bytes(send_b.at[unit, pl.ds(0, N - slabs)], b_send.at[unit])
    wait_bytes(precv.at[pl.ds(0, n_grid - 1)], p_send)


def per_device(n_band, n_grid, basis, rotation, ritz_values, potential, col_map):
    n_sub = basis.shape[0]
    total = col_map.shape[0]
    slabs = N // n_grid
    inverse_z, forward_z, tables = make_tables()
    in_vmem = pl.BlockSpec(memory_space=pltpu.VMEM)
    in_smem = pl.BlockSpec(memory_space=pltpu.SMEM)
    own = (2, N, N)
    wide = (2 * slabs * LOW, total)
    rows = (slabs * N, 2 * N)
    cols = (2 * N, slabs * N)
    read = (2 * slabs * LOW, TOP * N)
    dma = pltpu.SemaphoreType.DMA
    resid, h_resid, inter = pl.pallas_call(
        functools.partial(kernel, n_band, n_grid, total),
        out_shape=(
            jax.ShapeDtypeStruct(own, F32),
            jax.ShapeDtypeStruct(own, F32),
            jax.ShapeDtypeStruct((n_sub, 2 * n_band), F32),
        ),
        in_specs=[in_vmem, in_smem, in_smem, in_vmem, in_vmem, in_vmem, in_vmem, in_vmem],
        out_specs=(in_vmem, in_vmem, in_vmem),
        scratch_shapes=[
            pltpu.VMEM((2, n_band, N, N), F32),
            pltpu.VMEM((2, n_band, N, N), F32),
            pltpu.VMEM((2, N, N), F32),
            pltpu.VMEM((N, N), F32),
            pltpu.VMEM((total, TOP * N), BF16),
            pltpu.VMEM((TOP * N, total), BF16),
            pltpu.VMEM((LOW, total), F32),
            pltpu.VMEM((N, N), F32),
            pltpu.VMEM((4, N, N), F32),
            pltpu.VMEM((4, N, N), F32),
            pltpu.VMEM((4, N, N), F32),
            pltpu.VMEM((4, N, N), F32),
            pltpu.VMEM((2 * slabs, total), F32),
            pltpu.VMEM(wide, BF16),
            pltpu.VMEM(wide, BF16),
            pltpu.VMEM(rows, BF16),
            pltpu.VMEM(rows, BF16),
            pltpu.VMEM(cols, BF16),
            pltpu.VMEM(cols, BF16),
            pltpu.VMEM(read, BF16),
            pltpu.VMEM(read, BF16),
            pltpu.VMEM((2, n_band, N, N), F32),
            pltpu.VMEM((2, n_band, n_sub, 8, N), F32),
            pltpu.VMEM((n_sub, N), F32),
            pltpu.VMEM((n_grid, n_sub, N), F32),
            dma((2,)), dma((2,)), dma((4,)), dma((4,)), dma((4,)), dma((4,)),
            dma((2,)), dma((2,)), dma, dma,
        ],
        compiler_params=pltpu.CompilerParams(
            collective_id=0, has_side_effects=True, vmem_limit_bytes=48 * 1024 * 1024
        ),
    )(
        basis.reshape(n_sub, N, N), rotation, ritz_values, potential,
        col_map.reshape(total // N, N), jnp.asarray(inverse_z), jnp.asarray(forward_z),
        jnp.asarray(tables),
    )
    shape = (2, 2, HALF, N)
    return resid.reshape(shape), h_resid.reshape(shape), inter


def solution(mesh):
    placed = (P("band", None, "grid", None), P(), P("band"), P("grid", None, None), P())
    return jax.shard_map(
        functools.partial(per_device, mesh.shape["band"], mesh.shape["grid"]),
        mesh=mesh,
        in_specs=placed,
        out_specs=(P("band", None, "grid", None), P("band", None, "grid", None), P("band", None)),
        check_vma=False,
    )
```

time: 333 us -> 79.5 us (0.24); the launches traced: 327 us -> 79.1 us
  waiting for transfers between devices: 103 us -> 0 us
  Pallas kernels: 0 us -> 70.4 us
  matrix products: 70.2 us -> 0 us
  blocking collectives: 44 us -> 0 us
  local copies, waits for them, and re-layouts: 43.8 us -> 8.02 us
  other arithmetic: 34.9 us -> 0 us
  starting transfers between devices: 16.5 us -> 0 us
  between operations: 14.7 us -> 0.68 us
    all_gather x2 -> x0, waiting for transfers between devices: 84.6 us -> none  [the longest x1 84.6 us: per_device(): lax.all_gather(basis, 'band', axis=0, tiled=True)]
    pallas_call x0 -> x1, Pallas kernels: none -> 70.4 us  [per_device(): pl.pallas_call(functools.partial(kernel, n_band, n_grid, total), out_shap...]
    dot_general x10 -> x0, matrix products: 70.2 us -> none  [the longest x2 28 us: apply_hamiltonian(): jnp.einsum('pqck,bpscm->bqskm', inverse_x, weighted, precision=highest)]
    psum x1 -> x0, blocking collectives: 33.4 us -> none  [per_device(): intersection = lax.psum(partial_sum, 'grid') / float(2 * N * total_columns)]
    unnamed x43 -> x18, local copies, waits for them, and re-layouts: 27.9 us -> 8.02 us
    all_to_all x3 -> x0, waiting for transfers between devices: 17.5 us -> none  [the longest x2 10.9 us: apply_hamiltonian(): lax.all_to_all(spread, 'grid', split_axis=2, concat_axis=3, tiled=True)]
    all_to_all x3 -> x0, starting transfers between devices: 16.4 us -> none  [the longest x2 12.1 us: apply_hamiltonian(): lax.all_to_all(spread, 'grid', split_axis=2, concat_axis=3, tiled=True)]
    all_to_all x1 -> x0, blocking collectives: 10.6 us -> none  [apply_hamiltonian(): lax.all_to_all(picked, 'grid', split_axis=3, concat_axis=2, tiled=True)]
  transfers between devices with their start and end apart: 5 -> 0, of which waited for: 4 -> 0; matrix products, arithmetic and copies ran while one was open for 20% -> 0% of each run, Pallas kernels for 0% -> 0%
where the time goes in v1:
time: 79.5 us; the launch traced here: 79.1 us
  Pallas kernels  70.4 us (89%)
  local copies, waits for them, and re-layouts  8.02 us (10%)
    pallas_call x1, Pallas kernels, per_device(): pl.pallas_call(functools.partial(kernel, n_band, n_grid, total), out_shap...  70.4 us
    unnamed x18, local copies, waits for them, and re-layouts  8.02 us

profile of v1, /device:TPU:1, one launch (start us, length us, event | category | flops | bytes accessed | tf_op | source)
XLA Modules:
  0.0 79.1 jit_solution(9230118771850067334)
XLA Ops:
  0.6 0.0 copy-start.5
  0.6 0.0 copy-start.6
  0.7 0.8 %copy.11.rot_ref = f32[128,16]{1,0:T(8,128)S(1)} copy(f32[128,16]{0,1:T(8,128)} %param.9) | data formatting | bytes 16384 | tf_op args[1]
  1.5 0.0 copy-done.5
  1.5 0.0 copy-done.6
  1.5 0.0 copy-start
  1.5 1.2 %copy-done = f32[16,2,64,128]{3,2,1,0:T(8,128)S(1)} copy-done((f32[16,2,64,128]{3,2,1,0:T(8,128)S(1)}, f32[16,2,64,128]{3,2,1,0:T(8,128)}, u32[]{:S(2)}) %copy-start) | copy-done | bytes 1048600
  2.7 0.0 copy-start.1
  2.7 1.2 %copy-done.1 = bf16[8,256,256]{2,1,0:T(8,128)(2,1)S(1)} copy-done((bf16[8,256,256]{2,1,0:T(8,128)(2,1)S(1)}, bf16[8,256,256]{2,1,0:T(8,128)(2,1)}, u32[]{:S(2)}) %copy-start.1) | copy-done | bytes 1048600
  3.9 0.0 copy-start.2
  3.9 1.0 %copy-done.2 = f32[8,128,128]{2,1,0:T(8,128)S(1)} copy-done((f32[8,128,128]{2,1,0:T(8,128)S(1)}, f32[8,128,128]{2,1,0:T(8,128)}, u32[]{:S(2)}) %copy-start.2) | copy-done | bytes 524312
  5.0 0.0 copy-start.3
  5.0 0.9 %copy-done.3 = f32[256,128]{1,0:T(8,128)S(1)} copy-done((f32[256,128]{1,0:T(8,128)S(1)}, f32[256,128]{1,0:T(8,128)}, u32[]{:S(2)}) %copy-start.3) | copy-done | bytes 131096
  5.9 0.0 copy-start.4
  5.9 0.9 %copy-done.4 = f32[128,256]{1,0:T(8,128)S(1)} copy-done((f32[128,256]{1,0:T(8,128)S(1)}, f32[128,256]{1,0:T(8,128)}, u32[]{:S(2)}) %copy-start.4) | copy-done | bytes 131096
  6.8 70.4 %shard_map.103 = (f32[2,128,128]{2,1,0:T(8,128)S(1)}, f32[2,128,128]{2,1,0:T(8,128)S(1)}, f32[16,16]{1,0:T(8,128)S(1)}) custom-call(f32[16,128,128]{2,1,0:T(8,128)S(1)} %bitcast.4, f32[128,16]{1,0:T(8,128)S(1)} %copy.11.rot_ref, f32[2]{0:T(128)S(1)} %copy-done.6, f32[8,128,128]{2,1,0:T(8,128)S(1)} %copy-done.2, s32[8,128]{1,0:T(8,128)S(1)} %bitcast.7, ...), custom_call_target="tpu_custom_call" | custom-call | tf_op jit(solution)/shard_map/pallas_call | solution.py:408
  77.2 0.7 copy.15
  77.9 0.7 copy.16
  78.5 0.6 copy.17
Async XLA Ops:
  0.6 0.8 %copy-start.5 = (s32[1024]{0:T(1024)S(1)}, s32[1024]{0:T(1024)}, u32[]{:S(2)}) copy-start(s32[1024]{0:T(1024)} %param.12) | copy-start | bytes 12292
  0.6 0.8 %copy-start.6 = (f32[2]{0:T(128)S(1)}, f32[2]{0:T(128)}, u32[]{:S(2)}) copy-start(f32[2]{0:T(128)} %ritz_val_ref.1) | copy-start | bytes 28
  1.5 1.2 %copy-start = (f32[16,2,64,128]{3,2,1,0:T(8,128)S(1)}, f32[16,2,64,128]{3,2,1,0:T(8,128)}, u32[]{:S(2)}) copy-start(f32[16,2,64,128]{3,2,1,0:T(8,128)} %param.8) | copy-start | bytes 3145732
  2.7 1.2 %copy-start.1 = (bf16[8,256,256]{2,1,0:T(8,128)(2,1)S(1)}, bf16[8,256,256]{2,1,0:T(8,128)(2,1)}, u32[]{:S(2)}) copy-start(bf16[8,256,256]{2,1,0:T(8,128)(2,1)} %constant.8.clone.tab_ref) | copy-start | bytes 3145732
  3.9 1.0 %copy-start.2 = (f32[8,128,128]{2,1,0:T(8,128)S(1)}, f32[8,128,128]{2,1,0:T(8,128)}, u32[]{:S(2)}) copy-start(f32[8,128,128]{2,1,0:T(8,128)} %pot_ref.1) | copy-start | bytes 1572868
  5.0 0.9 %copy-start.3 = (f32[256,128]{1,0:T(8,128)S(1)}, f32[256,128]{1,0:T(8,128)}, u32[]{:S(2)}) copy-start(f32[256,128]{1,0:T(8,128)} %constant.7.clone.tzf_ref) | copy-start | bytes 393220
  5.9 0.9 %copy-start.4 = (f32[128,256]{1,0:T(8,128)S(1)}, f32[128,256]{1,0:T(8,128)}, u32[]{:S(2)}) copy-start(f32[128,256]{1,0:T(8,128)} %constant.6.clone.tzi_ref) | copy-start | bytes 393220

commit v2 on v1

--- a/solution.py
+++ b/solution.py
@@ -15,6 +15,8 @@
 LOW = 32
 TOP = N // LOW
 KINETIC_COEF = 2.0
+PAIR = 2
+SIDE = 4
 F32 = jnp.float32
 BF16 = jnp.bfloat16
 
@@ -46,6 +48,30 @@
 RIGHT_INV, LEFT_INV, RIGHT_FWD, LEFT_FWD = 0, 2, 4, 6
 
 
+def grid_far(offset):
+    x = offset // 4
+    return (x if x < 3 else 1) + 2 * (offset // 2 % 2)
+
+
+def band_far(offset):
+    y = offset % 4
+    return (y if y < 3 else 1) + offset // 4
+
+
+def flip(index, offset):
+    bit = 1
+    while bit <= offset:
+        if offset & bit:
+            index = index + bit - 2 * bit * (index // bit % 2)
+        bit *= 2
+    return index
+
+
+def far_first(index, count, far):
+    order = sorted(range(1, count), key=lambda offset: -far(offset))
+    return [flip(index, offset) for offset in order]
+
+
 def split(value):
     high = value.astype(BF16)
     return high, (value - high.astype(F32)).astype(BF16)
@@ -61,12 +87,13 @@
 
 def kernel(
     n_band, n_grid, total,
-    basis_ref, rot_ref, ritz_val_ref, pot_ref, map_ref, tzi_ref, tzf_ref, tab_ref,
+    basis_in, rot_in, ritz_val_in, pot_in, map_in, tzi_in, tzf_in, tab_in,
     resid_ref, hres_ref, inter_ref,
     part, rs, coeff, kin, onehot, onehot_t, mask, tmp,
     send_f, recv_f, send_b, recv_b,
-    vals, wide_h, wide_l, rows_h, rows_l, cols_h, cols_l, read_h, read_l,
+    vals, wide, rows, read,
     gath, acc, psend, precv,
+    basis_ref, rot_ref, ritz_val_ref, pot_ref, map_ref, tzi_ref, tzf_ref, tab_ref, in_sems,
     rs_send, rs_recv, f_send, f_recv, b_send, b_recv, g_send, g_recv, p_send, p_recv,
 ):
     slabs = N // n_grid
@@ -75,6 +102,24 @@
     my_band = lax.axis_index("band")
     my_grid = lax.axis_index("grid")
 
+    loads = [
+        pltpu.make_async_copy(source, target, in_sems.at[k])
+        for k, (source, target) in enumerate(
+            (
+                (rot_in, rot_ref),
+                (basis_in, basis_ref),
+                (map_in, map_ref),
+                (tzi_in, tzi_ref),
+                (tab_in, tab_ref),
+                (pot_in, pot_ref),
+                (tzf_in, tzf_ref),
+                (ritz_val_in, ritz_val_ref),
+            )
+        )
+    ]
+    for load in loads:
+        load.start()
+
     barrier = pltpu.get_barrier_semaphore()
 
     def greet_band(step, carry):
@@ -89,20 +134,24 @@
 
     lax.fori_loop(1, n_band, greet_band, 0)
     lax.fori_loop(1, n_grid, greet_grid, 0)
-    pl.semaphore_wait(barrier, n_band - 1 + n_grid - 1)
 
     def partial_of(owner, which):
         column = owner * 2 + which
         row = my_band * n_sub
-        value = rot_ref[row, column] * basis_ref[0]
+        value = rot_ref[column, row] * basis_ref[0]
         for i in range(1, n_sub):
-            value = value + rot_ref[row + i, column] * basis_ref[i]
+            value = value + rot_ref[column, row + i] * basis_ref[i]
         return value
 
+    loads[0].wait()
+    loads[1].wait()
+    started = False
     for which in range(2):
-        def send_partial(step, carry, which=which):
-            owner = lax.rem(my_band + step, n_band)
+        for owner in far_first(my_band, n_band, band_far):
             part[which, owner] = partial_of(owner, which)
+            if not started:
+                pl.semaphore_wait(barrier, n_band - 1 + n_grid - 1)
+                started = True
             pltpu.make_async_remote_copy(
                 src_ref=part.at[which, owner],
                 dst_ref=rs.at[which, my_band],
@@ -111,10 +160,8 @@
                 device_id=(owner, my_grid),
                 device_id_type=MESH,
             ).start()
-            return carry
-
-        lax.fori_loop(1, n_band, send_partial, 0)
         rs[which, my_band] = partial_of(my_band, which)
+    loads[2].wait()
 
     lane_c = lax.broadcasted_iota(jnp.int32, (TOP * N, N), 0)
     lane_r = lax.broadcasted_iota(jnp.int32, (LOW, N), 0)
@@ -145,14 +192,16 @@
     kin[0:HALF] = kinetic
     kin[HALF:N] = kinetic
 
+    for load in loads[3:]:
+        load.wait()
+
     lane = lax.broadcasted_iota(jnp.int32, (slabs, N), 1)
     first = lane < HALF
 
     def exchange(send, recv, send_sem, recv_sem, unit):
-        def go(step, carry):
-            peer = lax.rem(my_grid + step, n_grid)
+        here_at = pl.multiple_of(my_grid * slabs, slabs)
+        for peer in far_first(my_grid, n_grid, grid_far):
             there = pl.multiple_of(peer * slabs, slabs)
-            here_at = pl.multiple_of(my_grid * slabs, slabs)
             pltpu.make_async_remote_copy(
                 src_ref=send.at[unit, pl.ds(there, slabs)],
                 dst_ref=recv.at[unit, pl.ds(here_at, slabs)],
@@ -161,10 +210,7 @@
                 device_id=(my_band, peer),
                 device_id_type=MESH,
             ).start()
-            return carry
-
-        lax.fori_loop(1, n_grid, go, 0)
-        own = pl.multiple_of(my_grid * slabs, slabs)
+        own = here_at
         recv[unit, pl.ds(own, slabs)] = send[unit, pl.ds(own, slabs)]
 
     def wait_exchange(recv, sem, unit):
@@ -189,7 +235,7 @@
         coeff[which] = value
         spread(value, which)
 
-    def plane_inverse(unit):
+    def place_values(unit):
         wait_exchange(recv_f, f_recv, unit)
         for j in range(chunks):
             span = slice(j * N, (j + 1) * N)
@@ -203,65 +249,75 @@
             high = row.astype(BF16).astype(F32)
             low = row - high
             span = slice(k * LOW, (k + 1) * LOW)
-            wide_h[span] = jnp.where(chosen, jnp.broadcast_to(high, chosen.shape), 0.0).astype(BF16)
-            wide_l[span] = jnp.where(chosen, jnp.broadcast_to(low, chosen.shape), 0.0).astype(BF16)
-        for wide, rows in ((wide_h, rows_h), (wide_l, rows_l)):
-            placed = dot(wide[...], onehot[...]).astype(BF16)
+            wide[span] = jnp.where(chosen, jnp.broadcast_to(high, chosen.shape), 0.0).astype(BF16)
+            span = slice((2 * slabs + k) * LOW, (2 * slabs + k + 1) * LOW)
+            wide[span] = jnp.where(chosen, jnp.broadcast_to(low, chosen.shape), 0.0).astype(BF16)
+
+    def place_columns():
+        placed = dot(wide[...], onehot[...]).astype(BF16)
+        for part_at in range(2):
             for q in range(2):
                 for s in range(slabs):
-                    k = q * slabs + s
+                    k = (part_at * 2 + q) * slabs + s
                     for t in range(TOP):
-                        rows[s * N + t * LOW:s * N + (t + 1) * LOW, q * N:(q + 1) * N] = placed[
-                            k * LOW:(k + 1) * LOW, t * N:(t + 1) * N
-                        ]
-        along_y = (
-            dot(rows_h[...], tab_ref[RIGHT_INV])
-            + dot(rows_h[...], tab_ref[RIGHT_INV + 1])
-            + dot(rows_l[...], tab_ref[RIGHT_INV])
-        )
-        high, low = split(along_y)
-        for q in range(2):
-            for s in range(slabs):
-                cols_h[q * N:(q + 1) * N, s * N:(s + 1) * N] = high[s * N:(s + 1) * N, q * N:(q + 1) * N]
-                cols_l[q * N:(q + 1) * N, s * N:(s + 1) * N] = low[s * N:(s + 1) * N, q * N:(q + 1) * N]
-        field = (
-            dot(tab_ref[LEFT_INV], cols_h[...])
-            + dot(tab_ref[LEFT_INV + 1], cols_h[...])
-            + dot(tab_ref[LEFT_INV], cols_l[...])
-        )
-        for s in range(slabs):
-            span = slice(s * N, (s + 1) * N)
-            here_pot = pot_ref[s]
-            for q in range(2):
-                high, low = split(field[q * N:(q + 1) * N, span] * here_pot)
-                cols_h[q * N:(q + 1) * N, span] = high
-                cols_l[q * N:(q + 1) * N, span] = low
-
-    def plane_forward(unit):
-        along_x = (
-            dot(tab_ref[LEFT_FWD], cols_h[...])
-            + dot(tab_ref[LEFT_FWD + 1], cols_h[...])
-            + dot(tab_ref[LEFT_FWD], cols_l[...])
-        )
-        high, low = split(along_x)
-        for q in range(2):
-            for s in range(slabs):
-                rows_h[s * N:(s + 1) * N, q * N:(q + 1) * N] = high[q * N:(q + 1) * N, s * N:(s + 1) * N]
-                rows_l[s * N:(s + 1) * N, q * N:(q + 1) * N] = low[q * N:(q + 1) * N, s * N:(s + 1) * N]
-        along_y = (
-            dot(rows_h[...], tab_ref[RIGHT_FWD])
-            + dot(rows_h[...], tab_ref[RIGHT_FWD + 1])
-            + dot(rows_l[...], tab_ref[RIGHT_FWD])
-        )
-        high, low = split(along_y)
-        for q in range(2):
-            for s in range(slabs):
-                k = q * slabs + s
-                for t in range(TOP):
-                    at = slice(s * N + t * LOW, s * N + (t + 1) * LOW)
-                    read_h[k * LOW:(k + 1) * LOW, t * N:(t + 1) * N] = high[at, q * N:(q + 1) * N]
-                    read_l[k * LOW:(k + 1) * LOW, t * N:(t + 1) * N] = low[at, q * N:(q + 1) * N]
-        picked = dot(read_h[...], onehot_t[...]) + dot(read_l[...], onehot_t[...])
+                        rows[
+                            s * N + t * LOW:s * N + (t + 1) * LOW,
+                            (part_at * 2 + q) * N:(part_at * 2 + q + 1) * N,
+                        ] = placed[k * LOW:(k + 1) * LOW, t * N:(t + 1) * N]
+
+    def right_table(which, high, low):
+        return dot(
+            jnp.concatenate([high, low, high], axis=1),
+            jnp.concatenate([tab_ref[which], tab_ref[which], tab_ref[which + 1]], axis=0),
+        )
+
+    def left_table(which, high, low):
+        return dot(
+            jnp.concatenate([tab_ref[which], tab_ref[which], tab_ref[which + 1]], axis=1),
+            jnp.concatenate([high, low, high], axis=0),
+        )
+
+    def turn(value, to_columns):
+        count = value.shape[0 if to_columns else 1] // N
+        if to_columns:
+            pieces = [[value[s * N:(s + 1) * N, q * N:(q + 1) * N] for s in range(count)] for q in range(2)]
+        else:
+            pieces = [[value[q * N:(q + 1) * N, s * N:(s + 1) * N] for q in range(2)] for s in range(count)]
+        return jnp.concatenate([jnp.concatenate(line, axis=1) for line in pieces], axis=0)
+
+    def transform():
+        def some(g, carry):
+            states = []
+            for h in range(SIDE):
+                at = (g * SIDE + h) * PAIR
+                piece = pl.ds(pl.multiple_of(at * N, N), PAIR * N)
+                states.append([rows[piece, 0:2 * N], rows[piece, 2 * N:4 * N]])
+            for h in range(SIDE):
+                states[h] = split(turn(right_table(RIGHT_INV, *states[h]), True))
+            for h in range(SIDE):
+                at = (g * SIDE + h) * PAIR
+                field = left_table(LEFT_INV, *states[h])
+                weights = jnp.concatenate([pot_ref[at + s] for s in range(PAIR)], axis=1)
+                states[h] = split(field * jnp.concatenate([weights, weights], axis=0))
+            for h in range(SIDE):
+                states[h] = split(turn(left_table(LEFT_FWD, *states[h]), False))
+            for h in range(SIDE):
+                at = (g * SIDE + h) * PAIR
+                both = split(right_table(RIGHT_FWD, *states[h]))
+                for p in range(2):
+                    for q in range(2):
+                        for s in range(PAIR):
+                            for t in range(TOP):
+                                read[
+                                    pl.ds(pl.multiple_of((q * slabs + at + s) * LOW, LOW), LOW),
+                                    (p * TOP + t) * N:(p * TOP + t + 1) * N,
+                                ] = both[p][s * N + t * LOW:s * N + (t + 1) * LOW, q * N:(q + 1) * N]
+            return carry
+
+        lax.fori_loop(0, slabs // (SIDE * PAIR), some, 0)
+
+    def read_columns(unit):
+        picked = dot(read[...], jnp.concatenate([onehot_t[...], onehot_t[...]], axis=0))
         for k in range(2 * slabs):
             vals[k:k + 1, :] = jnp.sum(
                 picked[k * LOW:(k + 1) * LOW] * mask[...], axis=0, keepdims=True
@@ -276,6 +332,12 @@
             send_b[unit, (2 * j + 1) * slabs:(2 * j + 2) * slabs] = jnp.where(
                 first, pltpu.roll(real, HALF, 1), imag
             )
+
+    def plane(unit):
+        place_values(unit)
+        place_columns()
+        transform()
+        read_columns(unit)
         exchange(send_b, recv_b, b_send, b_recv, unit)
 
     def finish(unit, which):
@@ -299,22 +361,33 @@
         gath[which, my_band] = value
         spread(value, unit + 2)
 
-        def go(step, carry):
-            owner = lax.rem(my_band + step, n_band)
-            pltpu.make_async_remote_copy(
-                src_ref=gath.at[which, my_band],
-                dst_ref=gath.at[which, my_band],
-                send_sem=g_send.at[which],
-                recv_sem=g_recv.at[which],
-                device_id=(owner, my_grid),
-                device_id_type=MESH,
-            ).start()
-            return carry
-
-        lax.fori_loop(1, n_band, go, 0)
+
+    def gather_copy(which, block, owner, sems):
+        return pltpu.make_async_remote_copy(
+            src_ref=gath.at[which, block],
+            dst_ref=gath.at[which, block],
+            send_sem=g_send.at[which, sems],
+            recv_sem=g_recv.at[which, sems],
+            device_id=(owner, my_grid),
+            device_id_type=MESH,
+        )
+
+    ring = n_band // 2
+    across = flip(my_band, ring)
+
+    def gather_own(which):
+        gather_copy(which, my_band, across, 0).start()
+        for offset in range(ring - 1, 0, -1):
+            gather_copy(which, my_band, flip(my_band, offset), 1).start()
+
+    def gather_across(which):
+        wait_bytes(gath.at[which, 0], g_recv.at[which, 0])
+        for offset in range(ring - 1, 0, -1):
+            gather_copy(which, across, flip(my_band, offset), 2).start()
 
     def products(which):
-        wait_bytes(gath.at[which, pl.ds(0, n_band - 1)], g_recv.at[which])
+        for sems in (1, 2):
+            wait_bytes(gath.at[which, pl.ds(0, ring - 1)], g_recv.at[which, sems])
 
         def of_owner(owner, carry):
             there = gath[which, owner]
@@ -343,8 +416,7 @@
         psend[...] = total_sum
         precv[my_grid] = total_sum
 
-        def go(step, carry):
-            peer = lax.rem(my_grid + step, n_grid)
+        for peer in far_first(my_grid, n_grid, grid_far):
             pltpu.make_async_remote_copy(
                 src_ref=psend,
                 dst_ref=precv.at[my_grid],
@@ -353,39 +425,35 @@
                 device_id=(my_band, peer),
                 device_id_type=MESH,
             ).start()
-            return carry
-
-        lax.fori_loop(1, n_grid, go, 0)
 
     ritz_ready(0)
-    plane_inverse(0)
     ritz_ready(1)
-    plane_forward(0)
-
-    plane_inverse(1)
+    plane(0)
+    plane(1)
     residual(0)
-    plane_forward(1)
-
-    plane_inverse(2)
+    gather_own(0)
     residual(1)
-    plane_forward(2)
-
-    plane_inverse(3)
+    gather_own(1)
+    gather_across(0)
+    plane(2)
+    gather_across(1)
+    plane(3)
     hres_ref[0] = finish(2, 0)
     products(0)
     products(1)
     send_products()
-    plane_forward(3)
+    hres_ref[1] = finish(3, 1)
     wait_bytes(precv.at[pl.ds(0, n_grid - 1)], p_recv)
     value = precv[0]
     for d in range(1, n_grid):
         value = value + precv[d]
     inter_ref[...] = value[:, 0:2 * n_band] / float(2 * N * total)
-    hres_ref[1] = finish(3, 1)
 
     for which in range(2):
         wait_bytes(part.at[which, pl.ds(0, n_band - 1)], rs_send.at[which])
-        wait_bytes(gath.at[which, pl.ds(0, n_band - 1)], g_send.at[which])
+        wait_bytes(gath.at[which, 0], g_send.at[which, 0])
+        for sems in (1, 2):
+            wait_bytes(gath.at[which, pl.ds(0, ring - 1)], g_send.at[which, sems])
     for unit in range(4):
         wait_bytes(send_f.at[unit, pl.ds(0, N - slabs)], f_send.at[unit])
         wait_bytes(send_b.at[unit, pl.ds(0, N - slabs)], b_send.at[unit])
@@ -398,12 +466,11 @@
     slabs = N // n_grid
     inverse_z, forward_z, tables = make_tables()
     in_vmem = pl.BlockSpec(memory_space=pltpu.VMEM)
-    in_smem = pl.BlockSpec(memory_space=pltpu.SMEM)
+    in_hbm = pl.BlockSpec(memory_space=pltpu.HBM)
     own = (2, N, N)
-    wide = (2 * slabs * LOW, total)
-    rows = (slabs * N, 2 * N)
-    cols = (2 * N, slabs * N)
-    read = (2 * slabs * LOW, TOP * N)
+    wide = (4 * slabs * LOW, total)
+    rows = (slabs * N, 4 * N)
+    read = (2 * slabs * LOW, 2 * TOP * N)
     dma = pltpu.SemaphoreType.DMA
     resid, h_resid, inter = pl.pallas_call(
         functools.partial(kernel, n_band, n_grid, total),
@@ -412,7 +479,7 @@
             jax.ShapeDtypeStruct(own, F32),
             jax.ShapeDtypeStruct((n_sub, 2 * n_band), F32),
         ),
-        in_specs=[in_vmem, in_smem, in_smem, in_vmem, in_vmem, in_vmem, in_vmem, in_vmem],
+        in_specs=[in_hbm] * 8,
         out_specs=(in_vmem, in_vmem, in_vmem),
         scratch_shapes=[
             pltpu.VMEM((2, n_band, N, N), F32),
@@ -429,25 +496,29 @@
             pltpu.VMEM((4, N, N), F32),
             pltpu.VMEM((2 * slabs, total), F32),
             pltpu.VMEM(wide, BF16),
-            pltpu.VMEM(wide, BF16),
             pltpu.VMEM(rows, BF16),
-            pltpu.VMEM(rows, BF16),
-            pltpu.VMEM(cols, BF16),
-            pltpu.VMEM(cols, BF16),
-            pltpu.VMEM(read, BF16),
             pltpu.VMEM(read, BF16),
             pltpu.VMEM((2, n_band, N, N), F32),
             pltpu.VMEM((2, n_band, n_sub, 8, N), F32),
             pltpu.VMEM((n_sub, N), F32),
             pltpu.VMEM((n_grid, n_sub, N), F32),
+            pltpu.VMEM((n_sub, N, N), F32),
+            pltpu.SMEM((2 * n_band, n_band * n_sub), F32),
+            pltpu.SMEM((2,), F32),
+            pltpu.VMEM((slabs, N, N), F32),
+            pltpu.VMEM((total // N, N), jnp.int32),
+            pltpu.VMEM((N, 2 * N), F32),
+            pltpu.VMEM((2 * N, N), F32),
+            pltpu.VMEM((8, 2 * N, 2 * N), BF16),
+            dma((8,)),
             dma((2,)), dma((2,)), dma((4,)), dma((4,)), dma((4,)), dma((4,)),
-            dma((2,)), dma((2,)), dma, dma,
+            dma((2, 3)), dma((2, 3)), dma, dma,
         ],
         compiler_params=pltpu.CompilerParams(
-            collective_id=0, has_side_effects=True, vmem_limit_bytes=48 * 1024 * 1024
+            collective_id=0, has_side_effects=True, vmem_limit_bytes=56 * 1024 * 1024
         ),
     )(
-        basis.reshape(n_sub, N, N), rotation, ritz_values, potential,
+        basis.reshape(n_sub, N, N), rotation.T, ritz_values, potential,
         col_map.reshape(total // N, N), jnp.asarray(inverse_z), jnp.asarray(forward_z),
         jnp.asarray(tables),
     )

time: 79.5 us -> 59.1 us (0.74)
  Pallas kernels: 70.4 us -> 55.3 us
  local copies, waits for them, and re-layouts: 8.02 us -> 2.9 us
    pallas_call x1, Pallas kernels: 70.4 us -> 55.3 us  [per_device(): pl.pallas_call(functools.partial(kernel, n_band, n_grid, total), out_shap...]
    unnamed x18 -> x7, local copies, waits for them, and re-layouts: 8.02 us -> 2.9 us
where the time goes in v2:
time: 59.1 us; the launch traced here: 58.9 us
  Pallas kernels  55.3 us (94%)
  local copies, waits for them, and re-layouts  2.9 us (5%)
  between operations  0.65 us (1%)
    pallas_call x1, Pallas kernels, per_device(): pl.pallas_call(functools.partial(kernel, n_band, n_grid, total), out_shap...  55.3 us
    unnamed x7, local copies, waits for them, and re-layouts  2.9 us

profile of v2, /device:TPU:1, one launch (start us, length us, event | category | flops | bytes accessed | tf_op | source)
XLA Modules:
  0.0 58.9 jit_solution(13173679658087735646)
XLA Ops:
  0.6 55.3 %shard_map.103 = (f32[2,128,128]{2,1,0:T(8,128)}, f32[2,128,128]{2,1,0:T(8,128)}, f32[16,16]{1,0:T(8,128)}) custom-call(f32[16,128,128]{2,1,0:T(8,128)} %bitcast.5, f32[16,128]{1,0:T(8,128)} %bitcast.8, f32[2]{0:T(128)} %ritz_val_in.1, f32[8,128,128]{2,1,0:T(8,128)} %pot_in.1, s32[8,128]{1,0:T(8,128)} %bitcast.9, f32[128,256]{1,0:T(8,128)} %constant.6.clone.tzi_in, ...), custom_call_target="tpu_custom_call" | custom-call | tf_op jit(solution)/shard_map/pallas_call | solution.py:475
  56.0 0.0 copy-start
  56.0 1.6 %copy.14 = f32[2,2,64,128]{3,2,1,0:T(8,128)} copy(f32[2,2,64,128]{3,2,1,0:T(8,128)} %bitcast.7) | data formatting | bytes 262144
  57.6 0.0 copy-done
  57.6 0.0 copy-start.1
  57.6 0.7 %copy.15 = f32[2,2,64,128]{3,2,1,0:T(8,128)} copy(f32[2,2,64,128]{3,2,1,0:T(8,128)S(1)} %bitcast.6) | data formatting | bytes 262144
  58.3 0.0 copy-done.1
  58.3 0.6 %copy.16 = f32[16,16]{1,0:T(8,128)} copy(f32[16,16]{1,0:T(8,128)S(1)} %copy-done.1) | data formatting | bytes 2048
Async XLA Ops:
  56.0 1.6 %copy-start = (f32[2,128,128]{2,1,0:T(8,128)S(1)}, f32[2,128,128]{2,1,0:T(8,128)}, u32[]{:S(2)}) copy-start(f32[2,128,128]{2,1,0:T(8,128)} %get-tuple-element.7) | copy-start | bytes 393220
  57.6 0.7 %copy-start.1 = (f32[16,16]{1,0:T(8,128)S(1)}, f32[16,16]{1,0:T(8,128)}, u32[]{:S(2)}) copy-start(f32[16,16]{1,0:T(8,128)} %get-tuple-element.14) | copy-start | bytes 3076

commit v3 on v2

--- a/solution.py
+++ b/solution.py
@@ -35,8 +35,10 @@
 
 def make_tables():
     cosine, sine = angle_tables()
-    inverse_z = (np.concatenate([cosine, sine], axis=1) / N).astype(np.float32)
-    forward_z = np.concatenate([cosine, sine], axis=0).astype(np.float32)
+    high, low = split_table(np.concatenate([cosine, sine], axis=1) / N)
+    inverse_z = np.concatenate([high, low, high], axis=1)
+    high, low = split_table(np.concatenate([cosine, sine], axis=0))
+    forward_z = np.concatenate([high, low, high], axis=0)
     inverse = np.block([[cosine, sine], [-sine, cosine]]) / N
     forward = np.block([[cosine, -sine], [sine, cosine]])
     tables = np.concatenate(
@@ -88,7 +90,8 @@
 def kernel(
     n_band, n_grid, total,
     basis_in, rot_in, ritz_val_in, pot_in, map_in, tzi_in, tzf_in, tab_in,
-    resid_ref, hres_ref, inter_ref,
+    resid_out, hres_out, inter_out,
+    hres_ref, inter_ref, out_sems,
     part, rs, coeff, kin, onehot, onehot_t, mask, tmp,
     send_f, recv_f, send_b, recv_b,
     vals, wide, rows, read,
@@ -117,9 +120,6 @@
             )
         )
     ]
-    for load in loads:
-        load.start()
-
     barrier = pltpu.get_barrier_semaphore()
 
     def greet_band(step, carry):
@@ -134,6 +134,8 @@
 
     lax.fori_loop(1, n_band, greet_band, 0)
     lax.fori_loop(1, n_grid, greet_grid, 0)
+    for load in loads:
+        load.start()
 
     def partial_of(owner, which):
         column = owner * 2 + which
@@ -221,9 +223,10 @@
         right = jnp.concatenate(
             [jnp.concatenate([real, -imag], axis=1), jnp.concatenate([imag, real], axis=1)], axis=0
         )
+        high, low = split(right)
         send_f[unit] = lax.dot_general(
-            tzi_ref[...], right, (((1,), (1,)), ((), ())),
-            precision=lax.Precision.HIGHEST, preferred_element_type=F32,
+            tzi_ref[...], jnp.concatenate([high, high, low], axis=1), (((1,), (1,)), ((), ())),
+            preferred_element_type=F32,
         )
         exchange(send_f, recv_f, f_send, f_recv, unit)
 
@@ -333,12 +336,18 @@
                 first, pltpu.roll(real, HALF, 1), imag
             )
 
-    def plane(unit):
+    def plane_start(unit):
         place_values(unit)
         place_columns()
         transform()
+
+    def plane_end(unit):
         read_columns(unit)
         exchange(send_b, recv_b, b_send, b_recv, unit)
+
+    def plane(unit):
+        plane_start(unit)
+        plane_end(unit)
 
     def finish(unit, which):
         wait_exchange(recv_b, b_recv, unit)
@@ -347,9 +356,8 @@
         left = jnp.concatenate(
             [jnp.concatenate([real, imag], axis=1), jnp.concatenate([imag, -real], axis=1)], axis=0
         )
-        value = jnp.dot(
-            left, tzf_ref[...], precision=lax.Precision.HIGHEST, preferred_element_type=F32
-        )
+        high, low = split(left)
+        value = dot(jnp.concatenate([high, high, low], axis=1), tzf_ref[...])
         return value + kin[...] * coeff[which]
 
     def residual(unit):
@@ -357,9 +365,9 @@
         image = finish(unit, which)
         value = (image - ritz_val_ref[which] * coeff[which]) / (1.0 + kin[...])
         coeff[which] = value
-        resid_ref[which] = value
+        spread(value, unit + 2)
         gath[which, my_band] = value
-        spread(value, unit + 2)
+        pltpu.make_async_copy(gath.at[which, my_band], resid_out.at[which], out_sems.at[which]).start()
 
 
     def gather_copy(which, block, owner, sems):
@@ -389,30 +397,21 @@
         for sems in (1, 2):
             wait_bytes(gath.at[which, pl.ds(0, ring - 1)], g_recv.at[which, sems])
 
-        def of_owner(owner, carry):
+        lines = []
+        for owner in range(n_band):
             there = gath[which, owner]
             for i in range(n_sub):
-                both = basis_ref[i] * there
-                acc[which, owner, i] = jnp.sum(both.reshape(N // 8, 8, N), axis=0)
-            return carry
-
-        lax.fori_loop(0, n_band, of_owner, 0)
+                lines.append(jnp.sum(basis_ref[i] * there, axis=0, keepdims=True))
+        high, low = split(jnp.concatenate(lines, axis=0))
+        every = dot(jnp.concatenate([high, low], axis=1), jnp.ones((2 * N, N), BF16))
+        lanes = lax.broadcasted_iota(jnp.int32, (n_sub, N), 1)
+        found = jnp.zeros((n_sub, N), F32)
+        for owner in range(n_band):
+            found = jnp.where(lanes == 2 * owner + which, every[owner * n_sub:(owner + 1) * n_sub], found)
+        acc[which] = found
 
     def send_products():
-        count = 2 * n_band * n_sub
-        summed = jnp.sum(acc[...].reshape(count, 8, N), axis=1)
-        ones = jnp.ones((N, N), F32)
-        spread_sum = jnp.dot(
-            summed, ones, precision=lax.Precision.HIGHEST, preferred_element_type=F32
-        )
-        row = lax.broadcasted_iota(jnp.int32, (count, N), 0)
-        column = lax.broadcasted_iota(jnp.int32, (count, N), 1)
-        owner = lax.rem(row // n_sub, n_band)
-        which = row // (n_sub * n_band)
-        spread_sum = jnp.where(column == 2 * owner + which, spread_sum, 0.0)
-        total_sum = spread_sum[0:n_sub]
-        for k in range(1, 2 * n_band):
-            total_sum = total_sum + spread_sum[k * n_sub:(k + 1) * n_sub]
+        total_sum = acc[0] + acc[1]
         psend[...] = total_sum
         precv[my_grid] = total_sum
 
@@ -428,26 +427,39 @@
 
     ritz_ready(0)
     ritz_ready(1)
-    plane(0)
-    plane(1)
+    def first_planes(unit, carry):
+        plane(unit)
+        return carry
+
+    lax.fori_loop(0, 2, first_planes, 0)
     residual(0)
     gather_own(0)
+    gather_across(0)
     residual(1)
     gather_own(1)
-    gather_across(0)
-    plane(2)
-    gather_across(1)
-    plane(3)
-    hres_ref[0] = finish(2, 0)
+    def last_planes(unit, carry):
+        plane(unit)
+
+        @pl.when(unit == 2)
+        def _():
+            gather_across(1)
+
+        return carry
+
+    lax.fori_loop(2, 4, last_planes, 0)
     products(0)
     products(1)
     send_products()
+    hres_ref[0] = finish(2, 0)
+    pltpu.make_async_copy(hres_ref.at[0], hres_out.at[0], out_sems.at[2]).start()
     hres_ref[1] = finish(3, 1)
+    pltpu.make_async_copy(hres_ref.at[1], hres_out.at[1], out_sems.at[3]).start()
     wait_bytes(precv.at[pl.ds(0, n_grid - 1)], p_recv)
     value = precv[0]
     for d in range(1, n_grid):
         value = value + precv[d]
-    inter_ref[...] = value[:, 0:2 * n_band] / float(2 * N * total)
+    inter_ref[...] = value / float(2 * N * total)
+    pltpu.make_async_copy(inter_ref, inter_out, out_sems.at[4]).start()
 
     for which in range(2):
         wait_bytes(part.at[which, pl.ds(0, n_band - 1)], rs_send.at[which])
@@ -458,6 +470,31 @@
         wait_bytes(send_f.at[unit, pl.ds(0, N - slabs)], f_send.at[unit])
         wait_bytes(send_b.at[unit, pl.ds(0, N - slabs)], b_send.at[unit])
     wait_bytes(precv.at[pl.ds(0, n_grid - 1)], p_send)
+    for which in range(2):
+        pltpu.make_async_copy(gath.at[which, my_band], resid_out.at[which], out_sems.at[which]).wait()
+        pltpu.make_async_copy(hres_ref.at[which], hres_out.at[which], out_sems.at[2 + which]).wait()
+    pltpu.make_async_copy(inter_ref, inter_out, out_sems.at[4]).wait()
+
+
+def hand_out(resid_in, hres_in, inter_in, resid_out, hres_out, inter_out, held, held_inter, sems):
+    there = [
+        pltpu.make_async_copy(inter_in, held_inter, sems.at[0, 0]),
+        pltpu.make_async_copy(hres_in, held.at[0], sems.at[0, 1]),
+        pltpu.make_async_copy(resid_in, held.at[1], sems.at[0, 2]),
+    ]
+    back = [
+        pltpu.make_async_copy(held.at[0], hres_out, sems.at[1, 1]),
+        pltpu.make_async_copy(held.at[1], resid_out, sems.at[1, 2]),
+    ]
+    for copy in there:
+        copy.start()
+    there[0].wait()
+    inter_out[...] = held_inter[:, 0:inter_out.shape[1]]
+    for k in range(2):
+        there[1 + k].wait()
+        back[k].start()
+    for copy in back:
+        copy.wait()
 
 
 def per_device(n_band, n_grid, basis, rotation, ritz_values, potential, col_map):
@@ -477,11 +514,14 @@
         out_shape=(
             jax.ShapeDtypeStruct(own, F32),
             jax.ShapeDtypeStruct(own, F32),
-            jax.ShapeDtypeStruct((n_sub, 2 * n_band), F32),
+            jax.ShapeDtypeStruct((n_sub, N), F32),
         ),
         in_specs=[in_hbm] * 8,
-        out_specs=(in_vmem, in_vmem, in_vmem),
+        out_specs=(in_hbm, in_hbm, in_hbm),
         scratch_shapes=[
+            pltpu.VMEM((2, N, N), F32),
+            pltpu.VMEM((n_sub, N), F32),
+            dma((5,)),
             pltpu.VMEM((2, n_band, N, N), F32),
             pltpu.VMEM((2, n_band, N, N), F32),
             pltpu.VMEM((2, N, N), F32),
@@ -499,7 +539,7 @@
             pltpu.VMEM(rows, BF16),
             pltpu.VMEM(read, BF16),
             pltpu.VMEM((2, n_band, N, N), F32),
-            pltpu.VMEM((2, n_band, n_sub, 8, N), F32),
+            pltpu.VMEM((2, n_sub, N), F32),
             pltpu.VMEM((n_sub, N), F32),
             pltpu.VMEM((n_grid, n_sub, N), F32),
             pltpu.VMEM((n_sub, N, N), F32),
@@ -507,8 +547,8 @@
             pltpu.SMEM((2,), F32),
             pltpu.VMEM((slabs, N, N), F32),
             pltpu.VMEM((total // N, N), jnp.int32),
-            pltpu.VMEM((N, 2 * N), F32),
-            pltpu.VMEM((2 * N, N), F32),
+            pltpu.VMEM((N, 6 * N), BF16),
+            pltpu.VMEM((6 * N, N), BF16),
             pltpu.VMEM((8, 2 * N, 2 * N), BF16),
             dma((8,)),
             dma((2,)), dma((2,)), dma((4,)), dma((4,)), dma((4,)), dma((4,)),
@@ -522,6 +562,18 @@
         col_map.reshape(total // N, N), jnp.asarray(inverse_z), jnp.asarray(forward_z),
         jnp.asarray(tables),
     )
+    resid, h_resid, inter = pl.pallas_call(
+        hand_out,
+        out_shape=(
+            jax.ShapeDtypeStruct(own, F32),
+            jax.ShapeDtypeStruct(own, F32),
+            jax.ShapeDtypeStruct((n_sub, 2 * n_band), F32),
+        ),
+        in_specs=[in_hbm] * 3,
+        out_specs=(in_hbm, in_hbm, in_vmem),
+        scratch_shapes=[pltpu.VMEM((2,) + own, F32), pltpu.VMEM((n_sub, N), F32), dma((2, 3))],
+        compiler_params=pltpu.CompilerParams(vmem_limit_bytes=56 * 1024 * 1024),
+    )(resid, h_resid, inter)
     shape = (2, 2, HALF, N)
     return resid.reshape(shape), h_resid.reshape(shape), inter
 

time: 59.1 us -> 58.2 us (0.985)
  local copies, waits for them, and re-layouts: 2.9 us -> 0 us
  Pallas kernels: 55.3 us -> 57.3 us
    unnamed x7 -> x0, local copies, waits for them, and re-layouts: 2.9 us -> none
    pallas_call x0 -> x1, Pallas kernels: none -> 2.29 us  [per_device(): pl.pallas_call(hand_out, out_shape=(jax.ShapeDtypeStruct(own, F32), jax.S...]
where the time goes in v3:
time: 58.2 us; the launch traced here: 58 us
  Pallas kernels  57.3 us (98%)
  between operations  0.64 us (1%)
    pallas_call x1, Pallas kernels, per_device(): pl.pallas_call(functools.partial(kernel, n_band, n_grid, total), out_shap...  55 us
    pallas_call x1, Pallas kernels, per_device(): pl.pallas_call(hand_out, out_shape=(jax.ShapeDtypeStruct(own, F32), jax.S...  2.29 us

profile of v3, /device:TPU:1, one launch (start us, length us, event | category | flops | bytes accessed | tf_op | source)
XLA Modules:
  0.0 58.0 jit_solution(8088713935012642906)
XLA Ops:
  0.6 55.0 %shard_map.103 = (f32[2,128,128]{2,1,0:T(8,128)}, f32[2,128,128]{2,1,0:T(8,128)}, f32[16,128]{1,0:T(8,128)}) custom-call(f32[16,128,128]{2,1,0:T(8,128)} %bitcast.5, f32[16,128]{1,0:T(8,128)} %bitcast.6, f32[2]{0:T(128)} %ritz_val_in.1, f32[8,128,128]{2,1,0:T(8,128)} %pot_in.1, s32[8,128]{1,0:T(8,128)} %bitcast.7, bf16[128,768]{1,0:T(8,128)(2,1)} %constant.6.clone.tzi_in, ...), custom_call_target="tpu_custom_call" | custom-call | tf_op jit(solution)/shard_map/pallas_call | solution.py:512
  55.7 2.3 %shard_map.104 = (f32[2,128,128]{2,1,0:T(8,128)}, f32[2,128,128]{2,1,0:T(8,128)}, f32[16,16]{1,0:T(8,128)}) custom-call(f32[2,128,128]{2,1,0:T(8,128)} %get-tuple-element.9.resid_in, f32[2,128,128]{2,1,0:T(8,128)} %get-tuple-element.10.hres_in, f32[16,128]{1,0:T(8,128)} %get-tuple-element.11.inter_in), custom_call_target="tpu_custom_call" | custom-call | tf_op jit(solution)/shard_map/pallas_call | solution.py:565

commit v4 on v3

--- a/solution.py
+++ b/solution.py
@@ -95,7 +95,7 @@
     part, rs, coeff, kin, onehot, onehot_t, mask, tmp,
     send_f, recv_f, send_b, recv_b,
     vals, wide, rows, read,
-    gath, acc, psend, precv,
+    gath, psend, precv,
     basis_ref, rot_ref, ritz_val_ref, pot_ref, map_ref, tzi_ref, tzf_ref, tab_ref, in_sems,
     rs_send, rs_recv, f_send, f_recv, b_send, b_recv, g_send, g_recv, p_send, p_recv,
 ):
@@ -110,7 +110,6 @@
         for k, (source, target) in enumerate(
             (
                 (rot_in, rot_ref),
-                (basis_in, basis_ref),
                 (map_in, map_ref),
                 (tzi_in, tzi_ref),
                 (tab_in, tab_ref),
@@ -122,19 +121,20 @@
     ]
     barrier = pltpu.get_barrier_semaphore()
 
-    def greet_band(step, carry):
-        peer = lax.rem(my_band + step, n_band)
+    for peer in far_first(my_grid, n_grid, grid_far):
+        pl.semaphore_signal(barrier, inc=1, device_id=(my_band, peer), device_id_type=MESH)
+    for peer in far_first(my_band, n_band, band_far):
         pl.semaphore_signal(barrier, inc=1, device_id=(peer, my_grid), device_id_type=MESH)
-        return carry
-
-    def greet_grid(step, carry):
-        peer = lax.rem(my_grid + step, n_grid)
-        pl.semaphore_signal(barrier, inc=1, device_id=(my_band, peer), device_id_type=MESH)
-        return carry
-
-    lax.fori_loop(1, n_band, greet_band, 0)
-    lax.fori_loop(1, n_grid, greet_grid, 0)
-    for load in loads:
+    quarter = n_sub // 4
+    basis_loads = [
+        pltpu.make_async_copy(
+            basis_in.at[pl.ds(k * quarter, quarter)],
+            basis_ref.at[pl.ds(k * quarter, quarter)],
+            in_sems.at[len(loads) + k],
+        )
+        for k in range(4)
+    ]
+    for load in loads[:1] + basis_loads + loads[1:]:
         load.start()
 
     def partial_of(owner, which):
@@ -145,8 +145,8 @@
             value = value + rot_ref[column, row + i] * basis_ref[i]
         return value
 
-    loads[0].wait()
-    loads[1].wait()
+    for load in loads[:1] + basis_loads:
+        load.wait()
     started = False
     for which in range(2):
         for owner in far_first(my_band, n_band, band_far):
@@ -163,7 +163,7 @@
                 device_id_type=MESH,
             ).start()
         rs[which, my_band] = partial_of(my_band, which)
-    loads[2].wait()
+    loads[1].wait()
 
     lane_c = lax.broadcasted_iota(jnp.int32, (TOP * N, N), 0)
     lane_r = lax.broadcasted_iota(jnp.int32, (LOW, N), 0)
@@ -194,7 +194,7 @@
     kin[0:HALF] = kinetic
     kin[HALF:N] = kinetic
 
-    for load in loads[3:]:
+    for load in loads[2:]:
         load.wait()
 
     lane = lax.broadcasted_iota(jnp.int32, (slabs, N), 1)
@@ -393,25 +393,24 @@
         for offset in range(ring - 1, 0, -1):
             gather_copy(which, across, flip(my_band, offset), 2).start()
 
-    def products(which):
-        for sems in (1, 2):
-            wait_bytes(gath.at[which, pl.ds(0, ring - 1)], g_recv.at[which, sems])
-
+    def send_products():
+        for which in range(2):
+            for sems in (1, 2):
+                wait_bytes(gath.at[which, pl.ds(0, ring - 1)], g_recv.at[which, sems])
         lines = []
-        for owner in range(n_band):
-            there = gath[which, owner]
-            for i in range(n_sub):
-                lines.append(jnp.sum(basis_ref[i] * there, axis=0, keepdims=True))
+        for which in range(2):
+            for owner in range(n_band):
+                there = gath[which, owner]
+                for i in range(n_sub):
+                    lines.append(jnp.sum(basis_ref[i] * there, axis=0, keepdims=True))
         high, low = split(jnp.concatenate(lines, axis=0))
         every = dot(jnp.concatenate([high, low], axis=1), jnp.ones((2 * N, N), BF16))
         lanes = lax.broadcasted_iota(jnp.int32, (n_sub, N), 1)
-        found = jnp.zeros((n_sub, N), F32)
-        for owner in range(n_band):
-            found = jnp.where(lanes == 2 * owner + which, every[owner * n_sub:(owner + 1) * n_sub], found)
-        acc[which] = found
-
-    def send_products():
-        total_sum = acc[0] + acc[1]
+        total_sum = jnp.zeros((n_sub, N), F32)
+        for which in range(2):
+            for owner in range(n_band):
+                at = (which * n_band + owner) * n_sub
+                total_sum = jnp.where(lanes == 2 * owner + which, every[at:at + n_sub], total_sum)
         psend[...] = total_sum
         precv[my_grid] = total_sum
 
@@ -447,8 +446,6 @@
         return carry
 
     lax.fori_loop(2, 4, last_planes, 0)
-    products(0)
-    products(1)
     send_products()
     hres_ref[0] = finish(2, 0)
     pltpu.make_async_copy(hres_ref.at[0], hres_out.at[0], out_sems.at[2]).start()
@@ -539,7 +536,6 @@
             pltpu.VMEM(rows, BF16),
             pltpu.VMEM(read, BF16),
             pltpu.VMEM((2, n_band, N, N), F32),
-            pltpu.VMEM((2, n_sub, N), F32),
             pltpu.VMEM((n_sub, N), F32),
             pltpu.VMEM((n_grid, n_sub, N), F32),
             pltpu.VMEM((n_sub, N, N), F32),
@@ -550,7 +546,7 @@
             pltpu.VMEM((N, 6 * N), BF16),
             pltpu.VMEM((6 * N, N), BF16),
             pltpu.VMEM((8, 2 * N, 2 * N), BF16),
-            dma((8,)),
+            dma((11,)),
             dma((2,)), dma((2,)), dma((4,)), dma((4,)), dma((4,)), dma((4,)),
             dma((2, 3)), dma((2, 3)), dma, dma,
         ],

time: 58.2 us -> 58.7 us (level)
  Pallas kernels: 57.3 us -> 57.9 us
where the time goes in v4:
time: 58.7 us; the launch traced here: 58.5 us
  Pallas kernels  57.9 us (99%)
  between operations  0.64 us (1%)
    pallas_call x1, Pallas kernels, per_device(): pl.pallas_call(functools.partial(kernel, n_band, n_grid, total), out_shap...  55.6 us
    pallas_call x1, Pallas kernels, per_device(): pl.pallas_call(hand_out, out_shape=(jax.ShapeDtypeStruct(own, F32), jax.S...  2.29 us

profile of v4, /device:TPU:1, one launch (start us, length us, event | category | flops | bytes accessed | tf_op | source)
XLA Modules:
  0.0 58.5 jit_solution(9769251471419024807)
XLA Ops:
  0.6 55.6 %shard_map.103 = (f32[2,128,128]{2,1,0:T(8,128)}, f32[2,128,128]{2,1,0:T(8,128)}, f32[16,128]{1,0:T(8,128)}) custom-call(f32[16,128,128]{2,1,0:T(8,128)} %bitcast.5, f32[16,128]{1,0:T(8,128)} %bitcast.6, f32[2]{0:T(128)} %ritz_val_in.1, f32[8,128,128]{2,1,0:T(8,128)} %pot_in.1, s32[8,128]{1,0:T(8,128)} %bitcast.7, bf16[128,768]{1,0:T(8,128)(2,1)} %constant.6.clone.tzi_in, ...), custom_call_target="tpu_custom_call" | custom-call | tf_op jit(solution)/shard_map/pallas_call | solution.py:509
  56.2 2.3 %shard_map.104 = (f32[2,128,128]{2,1,0:T(8,128)}, f32[2,128,128]{2,1,0:T(8,128)}, f32[16,16]{1,0:T(8,128)}) custom-call(f32[2,128,128]{2,1,0:T(8,128)} %get-tuple-element.9.resid_in, f32[2,128,128]{2,1,0:T(8,128)} %get-tuple-element.10.hres_in, f32[16,128]{1,0:T(8,128)} %get-tuple-element.11.inter_in), custom_call_target="tpu_custom_call" | custom-call | tf_op jit(solution)/shard_map/pallas_call | solution.py:561

commit v5 on v3

--- a/solution.py
+++ b/solution.py
@@ -434,9 +434,9 @@
     lax.fori_loop(0, 2, first_planes, 0)
     residual(0)
     gather_own(0)
-    gather_across(0)
     residual(1)
     gather_own(1)
+    gather_across(0)
     def last_planes(unit, carry):
         plane(unit)
 

time: 58.2 us -> 58.1 us (level)
  no operation moved by 1% of the time
where the time goes in v5:
time: 58.1 us; the launch traced here: 57.9 us
  Pallas kernels  57.3 us (99%)
  between operations  0.64 us (1%)
    pallas_call x1, Pallas kernels, per_device(): pl.pallas_call(functools.partial(kernel, n_band, n_grid, total), out_shap...  55 us
    pallas_call x1, Pallas kernels, per_device(): pl.pallas_call(hand_out, out_shape=(jax.ShapeDtypeStruct(own, F32), jax.S...  2.29 us

profile of v5, /device:TPU:1, one launch (start us, length us, event | category | flops | bytes accessed | tf_op | source)
XLA Modules:
  0.0 57.9 jit_solution(4430615647888337062)
XLA Ops:
  0.6 55.0 %shard_map.103 = (f32[2,128,128]{2,1,0:T(8,128)}, f32[2,128,128]{2,1,0:T(8,128)}, f32[16,128]{1,0:T(8,128)}) custom-call(f32[16,128,128]{2,1,0:T(8,128)} %bitcast.5, f32[16,128]{1,0:T(8,128)} %bitcast.6, f32[2]{0:T(128)} %ritz_val_in.1, f32[8,128,128]{2,1,0:T(8,128)} %pot_in.1, s32[8,128]{1,0:T(8,128)} %bitcast.7, bf16[128,768]{1,0:T(8,128)(2,1)} %constant.6.clone.tzi_in, ...), custom_call_target="tpu_custom_call" | custom-call | tf_op jit(solution)/shard_map/pallas_call | solution.py:512
  55.6 2.3 %shard_map.104 = (f32[2,128,128]{2,1,0:T(8,128)}, f32[2,128,128]{2,1,0:T(8,128)}, f32[16,16]{1,0:T(8,128)}) custom-call(f32[2,128,128]{2,1,0:T(8,128)} %get-tuple-element.9.resid_in, f32[2,128,128]{2,1,0:T(8,128)} %get-tuple-element.10.hres_in, f32[16,128]{1,0:T(8,128)} %get-tuple-element.11.inter_in), custom_call_target="tpu_custom_call" | custom-call | tf_op jit(solution)/shard_map/pallas_call | solution.py:565
